TPU v7x, 32 devices: a whole 2x2x4 slice. The times are simulated.
32 devices in a mesh: dp: 8 (over z, x), tensor: 4 (over y, core).
Axes of the slice: x: 2, y: 2, z: 4, core: 2. Of those that a mesh axis runs over, the one named last changes fastest.
Arguments:
- tokens: bfloat16 [16, 1024, 768], P('dp', 'tensor'), may hold values from -6 to 6
- type_ids: int32 [16, 2], P('dp'), may hold values from 0 to 1
- boundary: int32 [16], P('dp'), may hold values from 128 to 896
- token_type_rows: float32 [2, 768], replicated, may hold values from -3 to 3
- query_key_value_weight: bfloat16 [768, 3, 768], P(None, None, 'tensor'), may hold values from -0.21875 to 0.21875
- b_qv: float32 [2, 768], P(None, 'tensor'), may hold values from -2 to 2
- output_weight: bfloat16 [768, 768], P('tensor'), may hold values from -0.875 to 0.875
- b_out: float32 [768], replicated, may hold values from -2 to 2
- gain_one: float32 [768], replicated, may hold values from 0.5 to 1.5
- shift_one: float32 [768], replicated, may hold values from -2 to 2
- gate_up_weight: bfloat16 [768, 2, 3072], P(None, None, 'tensor'), may hold values from -0.21875 to 0.21875
- gate_up_bias: float32 [2, 3072], P(None, 'tensor'), may hold values from -2 to 2
- down_weight: bfloat16 [3072, 768], P('tensor'), may hold values from -0.109375 to 0.109375
- b_down: float32 [768], replicated, may hold values from -2 to 2
- gain_two: float32 [768], replicated, may hold values from 0.5 to 1.5
- shift_two: float32 [768], replicated, may hold values from -2 to 2
- cotangent: bfloat16 [16, 1024, 768], P('dp', 'tensor'), may hold values from -6 to 6
Outputs:
- output: bfloat16 [16, 1024, 768], P('dp', 'tensor')
- grad_tokens: float32 [16, 1024, 768], P('dp', 'tensor')
- grad_type_table: float32 [2, 768], replicated
- grad_w_qkv: float32 [768, 3, 768], P(None, None, 'tensor')
- grad_b_qv: float32 [2, 768], P(None, 'tensor')
- grad_w_out: float32 [768, 768], P('tensor')
- grad_b_out: float32 [768], replicated
- grad_gain_one: float32 [768], replicated
- grad_shift_one: float32 [768], replicated
- grad_w_gu: float32 [768, 2, 3072], P(None, None, 'tensor')
- grad_b_gu: float32 [2, 3072], P(None, 'tensor')
- grad_w_down: float32 [3072, 768], P('tensor')
- grad_b_down: float32 [768], replicated
- grad_gain_two: float32 [768], replicated
- grad_shift_two: float32 [768], replicated
All inputs are finite; a program needn't handle non-finite values.
Results may differ from a plain program's by a relative error of at most 0.017.
The roundings to bfloat16 on the way count: a program that leaves them out, or rounds other values in their place, can miss the bound.
Values may be sent and summed in bfloat16 or wider, within the bound.
A program may use at most 192 MiB of HBM per device.

v0:
```python
from functools import partial

import jax
import jax.numpy as jnp
from jax import lax
from jax.sharding import PartitionSpec as P

HEADS = 12
HEAD_DIM = 64
MBATCH = 2


FULL_PRECISION = lax.Precision.HIGHEST
EPSILON = 1e-05


def layer_norm(values, scale_vec, shift_vec):
    center = jnp.mean(values, axis=-1, keepdims=True)
    centered = values - center
    spread = jnp.mean(centered * centered, axis=-1, keepdims=True)
    return centered * lax.rsqrt(spread + EPSILON) * scale_vec + shift_vec


def geglu(gate_up):
    return jax.nn.gelu(gate_up[..., 0, :], approximate=False) * gate_up[..., 1, :]


def score_block(queries, key_rows, slopes, distance):
    factor = queries.shape[-1] ** (-0.5)
    scores = (
        jnp.einsum("qhe,khe->hqk", queries, key_rows, preferred_element_type=jnp.float32) * factor
    )
    return scores - slopes[:, None, None] * distance


def attend_forward(blocks, slopes, distance):
    queries, key_rows, value_rows = blocks
    scores = score_block(queries, key_rows, slopes, distance)
    row_max = jnp.max(scores, axis=-1, keepdims=True)
    row_sum = jnp.sum(jnp.exp(scores - row_max), axis=-1, keepdims=True)
    log_total = row_max + jnp.log(row_sum)
    probs = jnp.exp(scores - log_total).astype(jnp.bfloat16)
    context = jnp.einsum("hqk,khe->qhe", probs, value_rows, preferred_element_type=jnp.float32)
    return (context, log_total)


def attend_backward(blocks, slopes, distance):
    queries, key_rows, value_rows, log_total, grad_context = blocks
    factor = queries.shape[-1] ** (-0.5)
    scores = score_block(queries, key_rows, slopes, distance)
    probs = jnp.exp(scores - log_total)
    probs_low = probs.astype(jnp.bfloat16)
    grad_values = jnp.einsum(
        "hqk,qhe->khe", probs_low, grad_context, preferred_element_type=jnp.float32
    )
    grad_probs = jnp.einsum(
        "qhe,khe->hqk", grad_context, value_rows, preferred_element_type=jnp.float32
    )
    inner = jnp.sum(grad_probs * probs, axis=-1, keepdims=True)
    grad_scores = (probs * (grad_probs - inner)).astype(jnp.bfloat16)
    grad_queries = (
        jnp.einsum("hqk,khe->qhe", grad_scores, key_rows, preferred_element_type=jnp.float32)
        * factor
    )
    grad_keys = (
        jnp.einsum("hqk,qhe->khe", grad_scores, queries, preferred_element_type=jnp.float32)
        * factor
    )
    return jnp.stack([grad_queries, grad_keys, grad_values], axis=1)


def per_device(
    tokens,
    type_ids,
    boundary,
    token_type_rows,
    query_key_value_weight,
    b_qv,
    output_weight,
    b_out,
    gain_one,
    shift_one,
    gate_up_weight,
    gate_up_bias,
    down_weight,
    b_down,
    gain_two,
    shift_two,
    cotangent,
):
    tensor_size = lax.axis_size("tensor")
    tensor_rank = lax.axis_index("tensor")
    seq_dev, rows_dev, width = tokens.shape
    length = rows_dev * tensor_size
    per_batch = seq_dev // MBATCH
    heads_dev = query_key_value_weight.shape[2] // HEAD_DIM
    type_range = jnp.arange(token_type_rows.shape[0])
    local_places = tensor_rank * rows_dev + jnp.arange(rows_dev)
    every_place = jnp.arange(length)
    distance = jnp.abs(every_place[:, None] - every_place[None, :]).astype(jnp.float32)
    head_ids = tensor_rank * heads_dev + jnp.arange(heads_dev)
    slopes = jnp.exp2(-8.0 * (head_ids + 1).astype(jnp.float32) / HEADS)
    bias_three = jnp.stack([b_qv[0], jnp.zeros_like(b_qv[0]), b_qv[1]])
    grad_table = jnp.zeros(token_type_rows.shape, jnp.float32)
    grad_w_qkv = jnp.zeros(query_key_value_weight.shape, jnp.float32)
    grad_b_qv = jnp.zeros(b_qv.shape, jnp.float32)
    grad_w_out = jnp.zeros(output_weight.shape, jnp.float32)
    grad_b_out = jnp.zeros(b_out.shape, jnp.float32)
    grad_gain_one = jnp.zeros(gain_one.shape, jnp.float32)
    grad_shift_one = jnp.zeros(shift_one.shape, jnp.float32)
    grad_w_gu = jnp.zeros(gate_up_weight.shape, jnp.float32)
    grad_b_gu = jnp.zeros(gate_up_bias.shape, jnp.float32)
    grad_w_down = jnp.zeros(down_weight.shape, jnp.float32)
    grad_b_down = jnp.zeros(b_down.shape, jnp.float32)
    grad_gain_two = jnp.zeros(gain_two.shape, jnp.float32)
    grad_shift_two = jnp.zeros(shift_two.shape, jnp.float32)
    output_parts = []
    grad_parts = []
    forward_attend = partial(attend_forward, slopes=slopes, distance=distance)
    backward_attend = partial(attend_backward, slopes=slopes, distance=distance)
    for micro_step in range(MBATCH):
        first = micro_step * per_batch
        token_matrix = tokens[first : first + per_batch].astype(jnp.float32)
        type_pair = type_ids[first : first + per_batch]
        bounds = boundary[first : first + per_batch]
        is_second = local_places[None, :] >= bounds[:, None]
        kind_ids = jnp.where(is_second, type_pair[:, 1:2], type_pair[:, 0:1])
        indicator_matrix = (kind_ids[..., None] == type_range).astype(jnp.float32)
        layer_input = token_matrix + jnp.einsum(
            "rbm,ma->rba", indicator_matrix, token_type_rows, precision=FULL_PRECISION
        )
        layer_input_rows = lax.all_gather(
            layer_input.astype(jnp.bfloat16), "tensor", axis=1, tiled=True
        )
        qkv_full = jnp.einsum(
            "ety,ykw->etkw",
            layer_input_rows,
            query_key_value_weight,
            preferred_element_type=jnp.float32,
        )
        qkv_low = (qkv_full + bias_three).astype(jnp.bfloat16)
        split_heads = qkv_low.reshape(per_batch, length, 3, heads_dev, HEAD_DIM)
        queries = split_heads[:, :, 0]
        key_rows = split_heads[:, :, 1]
        value_rows = split_heads[:, :, 2]
        context, log_total = lax.map(forward_attend, (queries, key_rows, value_rows))
        context_reduced = context.reshape(per_batch, length, -1).astype(jnp.bfloat16)
        attn_terms = jnp.einsum(
            "rma,ap->rmp", context_reduced, output_weight, preferred_element_type=jnp.float32
        )
        attn = lax.psum_scatter(attn_terms, "tensor", scatter_dimension=1, tiled=True)
        mixed = attn + b_out + layer_input
        normed, norm_one_back = jax.vjp(layer_norm, mixed, gain_one, shift_one)
        normalized_rows = lax.all_gather(normed.astype(jnp.bfloat16), "tensor", axis=1, tiled=True)
        gate_up = (
            jnp.einsum(
                "ety,ykw->etkw", normalized_rows, gate_up_weight, preferred_element_type=jnp.float32
            )
            + gate_up_bias
        )
        hidden, geglu_back = jax.vjp(geglu, gate_up)
        hidden_reduced = hidden.astype(jnp.bfloat16)
        ffn_terms = jnp.einsum(
            "rma,ap->rmp", hidden_reduced, down_weight, preferred_element_type=jnp.float32
        )
        ffn_out = lax.psum_scatter(ffn_terms, "tensor", scatter_dimension=1, tiled=True)
        second = ffn_out + b_down + normed
        result_rows, norm_two_back = jax.vjp(layer_norm, second, gain_two, shift_two)
        output_parts.append(result_rows.astype(jnp.bfloat16))
        grad_second, grad_g_two, grad_s_two = norm_two_back(
            cotangent[first : first + per_batch].astype(jnp.float32)
        )
        grad_gain_two = grad_gain_two + grad_g_two
        grad_shift_two = grad_shift_two + grad_s_two
        grad_b_down = grad_b_down + jnp.sum(grad_second, axis=(0, 1))
        feedforward_gradient = lax.all_gather(
            grad_second.astype(jnp.bfloat16), "tensor", axis=1, tiled=True
        )
        grad_hidden = jnp.einsum(
            "hex,wx->hew", feedforward_gradient, down_weight, preferred_element_type=jnp.float32
        )
        grad_w_down = grad_w_down + jnp.einsum(
            "bqa,bqe->ae", hidden_reduced, feedforward_gradient, preferred_element_type=jnp.float32
        )
        gate_up_gradient = geglu_back(grad_hidden)[0].astype(jnp.bfloat16)
        grad_b_gu = grad_b_gu + jnp.sum(gate_up_gradient, axis=(0, 1), dtype=jnp.float32)
        grad_w_gu = grad_w_gu + jnp.einsum(
            "vke,vkbw->ebw", normalized_rows, gate_up_gradient, preferred_element_type=jnp.float32
        )
        normed_terms = jnp.einsum(
            "xuqb,pqb->xup", gate_up_gradient, gate_up_weight, preferred_element_type=jnp.float32
        )
        grad_normed = grad_second + lax.psum_scatter(
            normed_terms, "tensor", scatter_dimension=1, tiled=True
        )
        grad_mixed, grad_g_one, grad_s_one = norm_one_back(grad_normed)
        grad_gain_one = grad_gain_one + grad_g_one
        grad_shift_one = grad_shift_one + grad_s_one
        grad_b_out = grad_b_out + jnp.sum(grad_mixed, axis=(0, 1))
        attention_gradient = lax.all_gather(
            grad_mixed.astype(jnp.bfloat16), "tensor", axis=1, tiled=True
        )
        grad_context = jnp.einsum(
            "hex,wx->hew", attention_gradient, output_weight, preferred_element_type=jnp.float32
        )
        grad_w_out = grad_w_out + jnp.einsum(
            "bqa,bqe->ae", context_reduced, attention_gradient, preferred_element_type=jnp.float32
        )
        grad_context = grad_context.astype(jnp.bfloat16).reshape(
            per_batch, length, heads_dev, HEAD_DIM
        )
        grad_heads = lax.map(
            backward_attend, (queries, key_rows, value_rows, log_total, grad_context)
        )
        query_key_value_gradient = grad_heads.reshape(per_batch, length, 3, -1).astype(jnp.bfloat16)
        column_sums = jnp.sum(query_key_value_gradient, axis=(0, 1), dtype=jnp.float32)
        grad_b_qv = grad_b_qv + jnp.stack([column_sums[0], column_sums[2]])
        grad_w_qkv = grad_w_qkv + jnp.einsum(
            "vke,vkbw->ebw",
            layer_input_rows,
            query_key_value_gradient,
            preferred_element_type=jnp.float32,
        )
        entered_terms = jnp.einsum(
            "xuqb,pqb->xup",
            query_key_value_gradient,
            query_key_value_weight,
            preferred_element_type=jnp.float32,
        )
        layer_input_gradient = grad_mixed + lax.psum_scatter(
            entered_terms.astype(jnp.bfloat16), "tensor", scatter_dimension=1, tiled=True
        ).astype(jnp.float32)
        grad_parts.append(layer_input_gradient)
        grad_table = grad_table + jnp.einsum(
            "ocj,och->jh", indicator_matrix, layer_input_gradient, precision=FULL_PRECISION
        )
    grad_w_qkv, grad_b_qv, grad_w_out, grad_w_gu, grad_b_gu, grad_w_down = lax.psum(
        (grad_w_qkv, grad_b_qv, grad_w_out, grad_w_gu, grad_b_gu, grad_w_down), "dp"
    )
    (
        grad_table,
        grad_b_out,
        grad_gain_one,
        grad_shift_one,
        grad_b_down,
        grad_gain_two,
        grad_shift_two,
    ) = lax.psum(
        (
            grad_table,
            grad_b_out,
            grad_gain_one,
            grad_shift_one,
            grad_b_down,
            grad_gain_two,
            grad_shift_two,
        ),
        ("dp", "tensor"),
    )
    output = jnp.concatenate(output_parts, axis=0)
    grad_tokens = jnp.concatenate(grad_parts, axis=0)
    return (
        output,
        grad_tokens,
        grad_table,
        grad_w_qkv,
        grad_b_qv,
        grad_w_out,
        grad_b_out,
        grad_gain_one,
        grad_shift_one,
        grad_w_gu,
        grad_b_gu,
        grad_w_down,
        grad_b_down,
        grad_gain_two,
        grad_shift_two,
    )


def solution(mesh):
    in_specs = (
        P("dp", "tensor", None),
        P("dp", None),
        P("dp"),
        P(),
        P(None, None, "tensor"),
        P(None, "tensor"),
        P("tensor", None),
        P(),
        P(),
        P(),
        P(None, None, "tensor"),
        P(None, "tensor"),
        P("tensor", None),
        P(),
        P(),
        P(),
        P("dp", "tensor", None),
    )
    out_specs = (
        P("dp", "tensor", None),
        P("dp", "tensor", None),
        P(),
        P(None, None, "tensor"),
        P(None, "tensor"),
        P("tensor", None),
        P(),
        P(),
        P(),
        P(None, None, "tensor"),
        P(None, "tensor"),
        P("tensor", None),
        P(),
        P(),
        P(),
    )
    return jax.shard_map(
        per_device, mesh=mesh, in_specs=in_specs, out_specs=out_specs, check_vma=False
    )
```

profile of v0, /device:TPU:0, one launch (start us, length us, event | category | flops | bytes accessed | tf_op | source)
XLA Modules:
  0.0 854.5 jit_solution(4030222991759248630)
XLA Ops:
  22.7 16.9 %all-gather.9.cloned.1.call-done = bf16[1,1024,768]{2,1,0:T(8,128)(2,1)} async-done(((bf16[1,256,768]{2,1,0:T(8,128)(2,1)}), bf16[1,1024,768]{2,1,0:T(8,128)(2,1)}) %all-gather.9.cloned.1.call-update) | async-done | bytes 1572880 | tf_op jit(solution)/shard_map/all_gather | solution.py:132
  43.5 17.9 %all-gather.13.cloned.1.call-done = bf16[1,1024,768]{2,1,0:T(8,128)(2,1)} async-done(((bf16[1,256,768]{2,1,0:T(8,128)(2,1)}), bf16[1,1024,768]{2,1,0:T(8,128)(2,1)}) %all-gather.13.cloned.1.call-update) | async-done | bytes 1572880 | tf_op jit(solution)/shard_map/all_gather | solution.py:132
  79.8 4.6 fusion.267
  95.0 22.6 %reduce-scatter.13.cloned.1.call-done = f32[1,256,768]{2,1,0:T(8,128)} async-done(((f32[1,1024,768]{2,1,0:T(8,128)}), f32[1,256,768]{2,1,0:T(8,128)}) %reduce-scatter.13.cloned.1.call-update) | async-done | bytes 786448 | tf_op jit(solution)/shard_map/reduce_scatter | solution.py:151
  117.6 41.1 %reduce-scatter.9.cloned.1.call-done = f32[1,256,768]{2,1,0:T(8,128)} async-done(((f32[1,1024,768]{2,1,0:T(8,128)}), f32[1,256,768]{2,1,0:T(8,128)}) %reduce-scatter.9.cloned.1.call-update) | async-done | bytes 786448 | tf_op jit(solution)/shard_map/reduce_scatter | solution.py:151
  163.9 18.8 %all-gather.15.cloned.1.call-done = bf16[1,1024,768]{2,1,0:T(8,128)(2,1)} async-done(((bf16[1,256,768]{2,1,0:T(8,128)(2,1)}), bf16[1,1024,768]{2,1,0:T(8,128)(2,1)}) %all-gather.15.cloned.1.call-update) | async-done | bytes 1572880 | tf_op jit(solution)/shard_map/all_gather | solution.py:154
  186.8 6.5 fusion.3
  198.3 6.1 all-gather.11.cloned.1.call-done
  208.5 6.5 fusion.2
  220.0 24.9 %reduce-scatter.15.cloned.1.call-done = f32[1,256,768]{2,1,0:T(8,128)} async-done(((f32[1,1024,768]{2,1,0:T(8,128)}), f32[1,256,768]{2,1,0:T(8,128)}) %reduce-scatter.15.cloned.1.call-update) | async-done | bytes 786448 | tf_op jit(solution)/shard_map/reduce_scatter | solution.py:166
  244.9 41.3 %reduce-scatter.11.cloned.1.call-done = f32[1,256,768]{2,1,0:T(8,128)} async-done(((f32[1,1024,768]{2,1,0:T(8,128)}), f32[1,256,768]{2,1,0:T(8,128)}) %reduce-scatter.11.cloned.1.call-update) | async-done | bytes 786448 | tf_op jit(solution)/shard_map/reduce_scatter | solution.py:166
  297.2 17.1 %all-gather.17.cloned.1.call-done = bf16[1,1024,768]{2,1,0:T(8,128)(2,1)} async-done(((bf16[1,256,768]{2,1,0:T(8,128)(2,1)}), bf16[1,1024,768]{2,1,0:T(8,128)(2,1)}) %all-gather.17.cloned.1.call-update) | async-done | bytes 1572880 | tf_op jit(solution)/shard_map/all_gather | solution.py:176
  314.2 6.8 multiply_bitcast_fusion.1
  328.1 7.8 all-gather.21.cloned.1.call-done
  335.9 6.8 multiply_bitcast_fusion
  351.3 5.5 fusion.12
  356.8 4.5 fusion.72
  361.3 15.1 %reduce-scatter.17.cloned.1.call-done = f32[1,256,768]{2,1,0:T(8,128)} async-done(((f32[1,1024,768]{2,1,0:T(8,128)}), f32[1,256,768]{2,1,0:T(8,128)}) %reduce-scatter.17.cloned.1.call-update) | async-done | bytes 786448 | tf_op jit(solution)/shard_map/reduce_scatter | solution.py:193
  376.4 40.5 %reduce-scatter.21.cloned.1.call-done = f32[1,256,768]{2,1,0:T(8,128)} async-done(((f32[1,1024,768]{2,1,0:T(8,128)}), f32[1,256,768]{2,1,0:T(8,128)}) %reduce-scatter.21.cloned.1.call-update) | async-done | bytes 786448 | tf_op jit(solution)/shard_map/reduce_scatter | solution.py:193
  422.1 11.1 %fusion.93 = f32[768,768]{1,0:T(8,128)} fusion(bf16[1,1024,768]{2,1,0:T(8,128)(2,1)} %all-gather.17.cloned.1.call-done, f32[1,1024,2,768]{3,1,2,0:T(8,128)} %copy-done.21), kind=kOutput, calls=%fused_computation.149 | convolution fusion | flops 1259864064 | bytes 10223616 | tf_op jit(solution)/shard_map/bqa,bqe->ae/dot_general | solution.py:182
  434.9 6.8 all-gather.19.cloned.1.call-done
  443.9 6.2 multiply_reduce_fusion.1
  452.7 5.3 multiply_convert_fusion.1
  458.0 5.0 fusion.137
  471.6 6.7 multiply_reduce_fusion
  480.8 5.3 multiply_convert_fusion
  486.0 5.0 fusion.139
  497.2 12.4 %fusion.122 = f32[768,768]{1,0:T(8,128)} fusion(f32[768,768]{1,0:T(8,128)} %fusion.93, bf16[1,1024,768]{2,1,0:T(8,128)(2,1)} %all-gather.21.cloned.1.call-done, f32[1,1024,2,768]{3,1,2,0:T(8,128)} %copy-done.20), kind=kOutput, calls=%fused_computation.177 | convolution fusion | flops 1260453888 | bytes 12582912 | tf_op jit(solution)/shard_map/bqa,bqe->ae/dot_general | solution.py:182
  527.7 22.6 %all-reduce.5 = (f32[2,192]{1,0:T(2,128)}, f32[2,768]{1,0:T(2,128)}) all-reduce(f32[2,192]{1,0:T(2,128)S(1)} %maximum_add_fusion, f32[2,768]{1,0:T(2,128)S(1)} %add.362), channel_id=1, replica_groups=mesh['dp'=8,'tensor'=4] {'dp'}, use_global_device_ids=true, to_apply=%region_34.35 | all-reduce | flops 1920 | bytes 15360 | tf_op jit(solution)/shard_map/psum | solution.py:237
  554.2 43.4 %all-reduce.4 = (f32[2,768]{1,0:T(2,128)}, f32[768]{0:T(1024)}, f32[768]{0:T(1024)}, f32[768]{0:T(1024)}, f32[768]{0:T(1024)}, /*index=5*/f32[768]{0:T(1024)}, f32[768]{0:T(1024)}) all-reduce(f32[2,768]{1,0:T(2,128)S(1)} %convolution_add_fusion, f32[768]{0:T(1024)S(1)} %copy-done.73, ...), channel_id=1, replica_groups=mesh['dp'=8,'tensor'=4] {'dp','tensor'}, use_global_device_ids=true, to_apply=%region_30.31 | all-reduce | flops 6144 | bytes 49152 | tf_op jit(solution)/shard_map/psum | solution.py:248
  598.8 236.5 %all-reduce.9.cloned.1.call-done = (f32[768,3,192]{0,2,1:T(8,128)}, f32[192,768]{1,0:T(8,128)}, f32[768,2,768]{2,0,1:T(8,128)}, f32[768,768]{1,0:T(8,128)}) async-done(((f32[768,3,192]{0,2,1:T(8,128)}, f32[192,768]{1,0:T(8,128)}, f32[768,2,768]{2,0,1:T(8,128)}, f32[768,768]{1,0:T(8,128)}), (f32[768,3,192]{0,2,1:T(8,128)}, f32[192,768]{1,0:T(8,128)}, f32[768,2,768]{2,0,1:T(8,128)}, ...) | async-done | bytes 9437200 | tf_op jit(solution)/shard_map/psum | solution.py:237
  835.3 8.3 copy.61
  (340 shorter events, 153.3 us)
Async XLA Ops:
  7.2 175.6 %copy-start = (bf16[768,2,768]{2,1,0:T(2,128)(2,1)S(1)}, bf16[768,2,768]{2,1,0:T(2,128)(2,1)}, u32[]{:S(2)}) copy-start(bf16[768,2,768]{2,1,0:T(2,128)(2,1)} %param.27) | copy-start | bytes 7077892
  7.2 32.4 %all-gather.9.cloned.1.call-start = ((), (), s32[]{:S(2)}) async-start(), calls=%async_computation.8 | async-start | bytes 1966080 | tf_op jit(solution)/shard_map/all_gather | solution.py:132
  17.1 22.5 %copy-start.92 = (bf16[768,3,192]{0,2,1:T(8,128)(2,1)S(1)}, bf16[768,3,192]{0,2,1:T(8,128)(2,1)}, u32[]{:S(2)}) copy-start(bf16[768,3,192]{0,2,1:T(8,128)(2,1)} %param.21) | copy-start | bytes 2654212
  17.1 44.3 %all-gather.13.cloned.1.call-start = ((), (), s32[]{:S(2)}) async-start(), calls=%async_computation.12 | async-start | bytes 1966080 | tf_op jit(solution)/shard_map/all_gather | solution.py:132
  19.8 97.8 %reduce-scatter.13.cloned.1.call-start = ((), (), s32[]{:S(2)}) async-start(), calls=%async_computation.13 | async-start | bytes 3932160 | tf_op jit(solution)/shard_map/reduce_scatter | solution.py:151
  79.5 79.2 %reduce-scatter.9.cloned.1.call-start = ((), (), s32[]{:S(2)}) async-start(), calls=%async_computation.9 | async-start | bytes 3932160 | tf_op jit(solution)/shard_map/reduce_scatter | solution.py:151
  92.6 66.0 %copy-start.84 = (f32[768]{0:T(1024)S(1)}, f32[768]{0:T(1024)}, u32[]{:S(2)}) copy-start(f32[768]{0:T(1024)} %param.24) | copy-start | bytes 9220
  94.9 87.8 %all-gather.15.cloned.1.call-start = ((), (), s32[]{:S(2)}) async-start(), calls=%async_computation.14 | async-start | bytes 1966080 | tf_op jit(solution)/shard_map/all_gather | solution.py:154
  162.9 41.5 %all-gather.11.cloned.1.call-start = ((), (), s32[]{:S(2)}) async-start(), calls=%async_computation.10 | async-start | bytes 1966080 | tf_op jit(solution)/shard_map/all_gather | solution.py:154
  163.5 81.4 %reduce-scatter.15.cloned.1.call-start = ((), (), s32[]{:S(2)}) async-start(), calls=%async_computation.15 | async-start | bytes 3932160 | tf_op jit(solution)/shard_map/reduce_scatter | solution.py:166
  198.2 87.9 %reduce-scatter.11.cloned.1.call-start = ((), (), s32[]{:S(2)}) async-start(), calls=%async_computation.11 | async-start | bytes 3932160 | tf_op jit(solution)/shard_map/reduce_scatter | solution.py:166
  219.8 66.4 %copy-start.86 = (f32[768]{0:T(1024)S(1)}, f32[768]{0:T(1024)}, u32[]{:S(2)}) copy-start(f32[768]{0:T(1024)} %param.30) | copy-start | bytes 9220
  219.8 69.1 %copy-start.61 = (f32[768]{0:T(1024)S(1)}, f32[768]{0:T(1024)}, u32[]{:S(2)}) copy-start(f32[768]{0:T(1024)} %param.31) | copy-start | bytes 9220
  219.8 94.4 %all-gather.17.cloned.1.call-start = ((), (), s32[]{:S(2)}) async-start(), calls=%async_computation.16 | async-start | bytes 1966080 | tf_op jit(solution)/shard_map/all_gather | solution.py:176
  294.4 41.5 %all-gather.21.cloned.1.call-start = ((), (), s32[]{:S(2)}) async-start(), calls=%async_computation.20 | async-start | bytes 1966080 | tf_op jit(solution)/shard_map/all_gather | solution.py:176
  297.1 79.3 %reduce-scatter.17.cloned.1.call-start = ((), (), s32[]{:S(2)}) async-start(), calls=%async_computation.17 | async-start | bytes 3932160 | tf_op jit(solution)/shard_map/reduce_scatter | solution.py:193
  328.1 88.9 %reduce-scatter.21.cloned.1.call-start = ((), (), s32[]{:S(2)}) async-start(), calls=%async_computation.21 | async-start | bytes 3932160 | tf_op jit(solution)/shard_map/reduce_scatter | solution.py:193
  349.9 91.9 %all-gather.19.cloned.1.call-start = ((), (), s32[]{:S(2)}) async-start(), calls=%async_computation.18 | async-start | bytes 1966080 | tf_op jit(solution)/shard_map/all_gather | solution.py:200
  356.8 60.2 %copy-start.8 = (f32[1,256,768]{2,1,0:T(8,128)S(1)}, f32[1,256,768]{2,1,0:T(8,128)}, u32[]{:S(2)}) copy-start(f32[1,256,768]{2,1,0:T(8,128)} %copy-done.7) | copy-start | bytes 2359300
  356.8 60.1 %copy-start.17 = (f32[1,256,768]{2,1,0:T(8,128)S(1)}, f32[1,256,768]{2,1,0:T(8,128)}, u32[]{:S(2)}) copy-start(f32[1,256,768]{2,1,0:T(8,128)} %get-tuple-element.187) | copy-start | bytes 2359300
  356.8 60.1 %copy-start.19 = (f32[1,256,768]{2,1,0:T(8,128)S(1)}, f32[1,256,768]{2,1,0:T(8,128)}, u32[]{:S(2)}) copy-start(f32[1,256,768]{2,1,0:T(8,128)} %copy-done.18) | copy-start | bytes 2359300
  422.0 47.4 %all-gather.23.cloned.1.call-start = ((), (), s32[]{:S(2)}) async-start(), calls=%async_computation.22 | async-start | bytes 1966080 | tf_op jit(solution)/shard_map/all_gather | solution.py:200
  434.6 115.7 %reduce-scatter.19.cloned.1.call-start = ((), (), s32[]{:S(2)}) async-start(), calls=%async_computation.19 | async-start | bytes 1966080 | tf_op jit(solution)/shard_map/reduce_scatter | solution.py:230
  464.2 45.4 %copy-start.28 = (bf16[3,64,1024]{2,1,0:T(8,128)(2,1)}, bf16[3,64,1024]{2,1,0:T(8,128)(2,1)S(1)}, u32[]{:S(2)}) copy-start(bf16[3,64,1024]{2,1,0:T(8,128)(2,1)S(1)} %fusion.136) | copy-start | bytes 1179652
  468.9 83.7 %reduce-scatter.23.cloned.1.call-start = ((), (), s32[]{:S(2)}) async-start(), calls=%async_computation.23 | async-start | bytes 1966080 | tf_op jit(solution)/shard_map/reduce_scatter | solution.py:230
  497.0 338.3 %all-reduce.9.cloned.1.call-start = ((), (), s32[]{:S(2)}) async-start(), calls=%async_computation.24 | async-start | bytes 18874368 | tf_op jit(solution)/shard_map/psum | solution.py:237
  524.7 25.7 %copy-start.16 = (f32[1,256,768]{2,1,0:T(8,128)S(1)}, f32[1,256,768]{2,1,0:T(8,128)}, u32[]{:S(2)}) copy-start(f32[1,256,768]{2,1,0:T(8,128)} %copy-done.15) | copy-start | bytes 2359300
  527.4 26.4 %copy-start.82 = (s32[256]{0:T(256)S(1)}, s32[256]{0:T(256)}, u32[]{:S(2)}) copy-start(s32[256]{0:T(256)} %copy-done.81) | copy-start | bytes 3076
  527.4 26.7 %copy-start.70 = (f32[768]{0:T(1024)S(1)}, f32[768]{0:T(1024)}, u32[]{:S(2)}) copy-start(f32[768]{0:T(1024)} %add.364) | copy-start | bytes 9220
  527.4 26.7 %copy-start.71 = (f32[768]{0:T(1024)S(1)}, f32[768]{0:T(1024)}, u32[]{:S(2)}) copy-start(f32[768]{0:T(1024)} %add.359) | copy-start | bytes 9220
  527.4 26.7 %copy-start.72 = (f32[768]{0:T(1024)S(1)}, f32[768]{0:T(1024)}, u32[]{:S(2)}) copy-start(f32[768]{0:T(1024)} %add.360) | copy-start | bytes 9220
  527.4 26.7 %copy-start.73 = (f32[768]{0:T(1024)S(1)}, f32[768]{0:T(1024)}, u32[]{:S(2)}) copy-start(f32[768]{0:T(1024)} %add.358) | copy-start | bytes 9220
  (87 other events, 371.0 us)
Sparse Core Ops, SparseCore 0:
  17.2 22.3 all-gather.8
  41.7 19.6 all-gather.12
  79.6 37.9 reduce-scatter.12
  120.7 37.9 reduce-scatter.8
  163.0 19.6 all-gather.14
  184.7 19.6 all-gather.10
  206.9 37.9 reduce-scatter.14
  248.2 37.9 reduce-scatter.10
  294.5 19.6 all-gather.16
  316.2 19.6 all-gather.20
  338.4 37.9 reduce-scatter.16
  379.0 37.9 reduce-scatter.20
  422.1 19.6 all-gather.18
  443.8 19.6 all-gather.22
  469.0 28.0 reduce-scatter.18
  500.2 28.1 reduce-scatter.22
  534.0 301.3 all-reduce.8
where the time goes:
time: 863 us; the launch traced here: 854 us
  waiting for transfers between devices  514 us (60%)
  matrix products  142 us (16%)
  other arithmetic  66.8 us (8%)
  blocking collectives  66 us (8%)
  local copies, waits for them, and re-layouts  47.7 us (6%)
  between operations  15.4 us (2%)
    psum x1, waiting for transfers between devices, per_device(): lax.psum((grad_w_qkv, grad_b_qv, grad_w_out, grad_w_gu, grad_b_gu, grad_w...  237 us
    reduce_scatter x2, waiting for transfers between devices, per_device(): lax.psum_scatter(ffn_terms, 'tensor', scatter_dimension=1, tiled=True)  66.1 us
    reduce_scatter x2, waiting for transfers between devices, per_device(): lax.psum_scatter(attn_terms, 'tensor', scatter_dimension=1, tiled=True)  63.7 us
    reduce_scatter x2, waiting for transfers between devices, per_device(): lax.psum_scatter(normed_terms, 'tensor', scatter_dimension=1, tiled=True)  55.6 us
    unnamed x208, local copies, waits for them, and re-layouts  44.8 us
    psum x1, blocking collectives, per_device(): lax.psum((grad_table, grad_b_out, grad_gain_one, grad_shift_one, grad_b_d...  43.4 us
    all_gather x2, waiting for transfers between devices, per_device(): lax.all_gather(layer_input.astype(jnp.bfloat16), 'tensor', axis=1, tiled=...  34.8 us
    all_gather x2, waiting for transfers between devices, per_device(): lax.all_gather(normed.astype(jnp.bfloat16), 'tensor', axis=1, tiled=True)  24.9 us
  transfers between devices with their start and end apart: 17, of which 14 were waited for; matrix products, arithmetic and copies ran while one was open for 20% of the time, Pallas kernels for 0%

commit v1 on v0

v1 whole, which is shorter than its diff:
```python
from functools import partial

import jax
import jax.numpy as jnp
from jax import lax
from jax.experimental import pallas as pl
from jax.experimental.pallas import tpu as pltpu
from jax.sharding import PartitionSpec as P

HEADS = 12
HEAD_DIM = 64
EPSILON = 1e-05
VMEM_LIMIT = 56 * 2**20
NT = (((1,), (1,)), ((), ()))
TN = (((0,), (0,)), ((), ()))
NN = (((1,), (0,)), ((), ()))


def dot(a, b, dims=NN):
    return lax.dot_general(a, b, dims, preferred_element_type=jnp.float32)


def fill_distance(base_ref, dist_ref):
    blocks = base_ref.shape[0]
    keys, queries = dist_ref.shape
    size = keys // blocks
    for kb in range(blocks):
        for qb in range(queries // size):
            row = lax.broadcasted_iota(jnp.int32, (size, size), 0) + base_ref[kb]
            col = lax.broadcasted_iota(jnp.int32, (size, size), 1) + base_ref[qb]
            dist_ref[kb * size : (kb + 1) * size, qb * size : (qb + 1) * size] = jnp.abs(
                row - col
            ).astype(jnp.float32)


def head_mask(shape, h):
    lane = lax.broadcasted_iota(jnp.int32, shape, 1)
    return (lane // HEAD_DIM) == h


def attention_forward_kernel(slope_ref, base_ref, q_ref, k_ref, v_ref, o_ref, lse_ref, dist_ref):
    pair = pl.program_id(0)

    @pl.when(pair == 0)
    def _():
        fill_distance(base_ref, dist_ref)

    k = k_ref[...]
    v = v_ref[...]
    q = q_ref[...]
    outs = []
    for h in range(2):
        qm = jnp.where(head_mask(q.shape, h), q, jnp.zeros_like(q)) * jnp.bfloat16(HEAD_DIM**-0.5)
        scores = dot(k, qm, NT) - slope_ref[2 * pair + h] * dist_ref[...]
        top = jnp.max(scores, axis=0, keepdims=True)
        p = jnp.exp(scores - top)
        total = jnp.sum(p, axis=0, keepdims=True)
        out = dot(v, p.astype(jnp.bfloat16), TN)
        outs.append(out[h * HEAD_DIM : (h + 1) * HEAD_DIM] / total)
        lse_ref[0, h : h + 1, :] = top + jnp.log(total)
    o_ref[...] = jnp.concatenate(outs, axis=0).T.astype(jnp.bfloat16)


def attention_forward(slopes, bases, q, k, v):
    rows, width = q.shape
    keys = k.shape[0]
    lanes = 2 * HEAD_DIM
    pairs = width // lanes
    return pl.pallas_call(
        attention_forward_kernel,
        grid=(pairs,),
        in_specs=[
            pl.BlockSpec(memory_space=pltpu.SMEM),
            pl.BlockSpec(memory_space=pltpu.SMEM),
            pl.BlockSpec((rows, lanes), lambda p: (0, p)),
            pl.BlockSpec((keys, lanes), lambda p: (0, p)),
            pl.BlockSpec((keys, lanes), lambda p: (0, p)),
        ],
        out_specs=[
            pl.BlockSpec((rows, lanes), lambda p: (0, p)),
            pl.BlockSpec((1, 2, rows), lambda p: (p, 0, 0)),
        ],
        out_shape=[
            jax.ShapeDtypeStruct((rows, width), jnp.bfloat16),
            jax.ShapeDtypeStruct((pairs, 2, rows), jnp.float32),
        ],
        scratch_shapes=[pltpu.VMEM((keys, rows), jnp.float32)],
        compiler_params=pltpu.CompilerParams(vmem_limit_bytes=VMEM_LIMIT),
        cost_estimate=pl.CostEstimate(
            flops=16 * rows * keys * width, bytes_accessed=12 * keys * width, transcendentals=0
        ),
    )(slopes, bases, q, k, v)


def attention_backward_kernel(
    slope_ref, base_ref, q_ref, k_ref, v_ref, do_ref, lse_ref, dq_ref, dk_ref, dv_ref, dist_ref
):
    pair = pl.program_id(0)

    @pl.when(pair == 0)
    def _():
        fill_distance(base_ref, dist_ref)

    k = k_ref[...]
    v = v_ref[...]
    q = q_ref[...]
    do = do_ref[...]
    dqs = []
    for h in range(2):
        mask = head_mask(q.shape, h)
        qm = jnp.where(mask, q, jnp.zeros_like(q)) * jnp.bfloat16(HEAD_DIM**-0.5)
        dom = jnp.where(mask, do, jnp.zeros_like(do))
        scores = dot(k, qm, NT) - slope_ref[2 * pair + h] * dist_ref[...]
        p = jnp.exp(scores - lse_ref[0, h : h + 1, :])
        dp = dot(v, dom, NT)
        inner = jnp.sum(p * dp, axis=0, keepdims=True)
        ds = (p * (dp - inner)).astype(jnp.bfloat16)
        dv = dot(p.astype(jnp.bfloat16), dom)
        dk = dot(ds, qm)
        if h == 0:
            dv_ref[...] = dv
            dk_ref[...] = dk
        else:
            dv_ref[...] += dv
            dk_ref[...] += dk
        dqs.append(dot(k, ds, TN)[h * HEAD_DIM : (h + 1) * HEAD_DIM])
    dq = jnp.concatenate(dqs, axis=0).T * (HEAD_DIM**-0.5)
    dq_ref[...] = dq.astype(jnp.bfloat16)


def attention_backward(slopes, bases, q, k, v, do, lse):
    rows, width = q.shape
    keys = k.shape[0]
    lanes = 2 * HEAD_DIM
    pairs = width // lanes
    row_spec = pl.BlockSpec((rows, lanes), lambda p: (0, p))
    key_spec = pl.BlockSpec((keys, lanes), lambda p: (0, p))
    return pl.pallas_call(
        attention_backward_kernel,
        grid=(pairs,),
        in_specs=[
            pl.BlockSpec(memory_space=pltpu.SMEM),
            pl.BlockSpec(memory_space=pltpu.SMEM),
            row_spec,
            key_spec,
            key_spec,
            row_spec,
            pl.BlockSpec((1, 2, rows), lambda p: (p, 0, 0)),
        ],
        out_specs=[row_spec, key_spec, key_spec],
        out_shape=[
            jax.ShapeDtypeStruct((rows, width), jnp.bfloat16),
            jax.ShapeDtypeStruct((keys, width), jnp.float32),
            jax.ShapeDtypeStruct((keys, width), jnp.float32),
        ],
        scratch_shapes=[pltpu.VMEM((keys, rows), jnp.float32)],
        compiler_params=pltpu.CompilerParams(vmem_limit_bytes=VMEM_LIMIT),
        cost_estimate=pl.CostEstimate(
            flops=40 * rows * keys * width, bytes_accessed=24 * keys * width, transcendentals=0
        ),
    )(slopes, bases, q, k, v, do, lse)


MESH = pl.DeviceIdType.MESH
UNITS = 8
WINDOW = 1


class Links:
    def __init__(self, ndp):
        self.ndp = ndp
        self.na = ndp // 2
        self.dp = lax.axis_index("dp")
        self.t = lax.axis_index("tensor")
        self.a = self.dp // 2
        self.b = lax.rem(self.dp, 2)
        self.y = self.t // 2
        self.c = lax.rem(self.t, 2)
        self.core = (self.dp, 2 * self.y + 1 - self.c)
        self.far = (self.dp, 2 * (1 - self.y) + self.c)
        self.pair = (2 * self.a + 1 - self.b, self.t)

    def up(self, off):
        return lax.rem(self.a + off, self.na)

    def down(self, off):
        return lax.rem(self.a + self.na - off, self.na)

    def column(self, off):
        return (2 * self.up(off) + self.b, self.t)

    def partners(self):
        return [self.core, self.far, self.pair] + [self.column(o) for o in range(1, self.na)]

    def greet(self):
        barrier = pltpu.get_barrier_semaphore()
        others = self.partners()
        for other in others:
            pl.semaphore_signal(barrier, inc=1, device_id=other, device_id_type=MESH)
        pl.semaphore_wait(barrier, len(others))


def remote(src, dst, send, recv, to):
    return pltpu.make_async_remote_copy(
        src_ref=src, dst_ref=dst, send_sem=send, recv_sem=recv, device_id=to, device_id_type=MESH
    )


def chunk_rows(ndp, rows):
    return -(-rows // (16 * ndp)) * 16


class Reducer:
    def __init__(self, links, refs, sems, rows, cols):
        self.l = links
        self.near, self.far, self.ybuf, self.xbuf, self.zbuf, self.own, self.fin = refs
        self.s = sems
        self.rows = rows
        self.cr = chunk_rows(links.ndp, rows)

    def clear_padding(self):
        padded = self.cr * self.l.ndp
        if padded > self.rows:
            self.near[:, self.rows :, :] = jnp.zeros_like(self.near[:, self.rows :, :])

    def at(self, ref, u, d):
        return ref.at[u, pl.ds(pl.multiple_of(d * self.cr, self.cr), self.cr)]

    def copy_y(self, u):
        s, r = self.s["y"]
        return remote(self.far.at[u], self.ybuf.at[u], s.at[u], r.at[u], self.l.far)

    def copy_x(self, u, i):
        s, r = self.s["x"]
        src = self.at(self.near, u, 2 * i + 1 - self.l.b)
        return remote(src, self.xbuf.at[u, i], s.at[u, i], r.at[u, i], self.l.pair)

    def copy_z(self, u, off):
        s, r = self.s["z"]
        src = self.at(self.near, u, 2 * self.l.up(off) + self.l.b)
        return remote(src, self.zbuf.at[u, off - 1], s.at[u, off - 1], r.at[u, off - 1], self.l.column(off))

    def copy_gz(self, u, off):
        s, r = self.s["gz"]
        dst = self.at(self.fin, u, self.l.dp)
        return remote(self.own.at[u], dst, s.at[u, off - 1], r.at[u, off - 1], self.l.column(off))

    def copy_gx(self, u, off):
        s, r = self.s["gx"]
        if off == 0:
            src, dst = self.own.at[u], self.at(self.fin, u, self.l.dp)
        else:
            d = 2 * self.l.down(off) + self.l.b
            src = dst = self.at(self.fin, u, d)
        return remote(src, dst, s.at[u, off], r.at[u, off], self.l.pair)

    def copy_own(self, u):
        return pltpu.make_async_copy(self.own.at[u], self.at(self.fin, u, self.l.dp), self.s["own"].at[u])

    def start_y(self, u):
        self.copy_y(u).start()

    def step_x(self, u):
        self.copy_y(u).wait_recv()
        if u + WINDOW < UNITS:
            self.start_y(u + WINDOW)
        f32 = jnp.float32
        rows = slice(0, self.rows)
        total = self.near[u, rows].astype(f32) + self.ybuf[u].astype(f32)
        self.near[u, rows] = total.astype(self.near.dtype)
        for i in range(self.l.na):
            self.copy_x(u, i).start()

    def step_z(self, u):
        f32 = jnp.float32
        for i in range(self.l.na):
            self.copy_x(u, i).wait_recv()
        for i in range(self.l.na):
            ref = self.at(self.near, u, 2 * i + self.l.b)
            ref[...] = (ref[...].astype(f32) + self.xbuf[u, i].astype(f32)).astype(self.near.dtype)
        for off in range(1, self.l.na):
            self.copy_z(u, off).start()

    def step_own(self, u):
        f32 = jnp.float32
        total = self.at(self.near, u, self.l.dp)[...].astype(f32)
        for off in range(1, self.l.na):
            self.copy_z(u, off).wait_recv()
            total = total + self.zbuf[u, off - 1].astype(f32)
        self.own[u] = total.astype(self.own.dtype)
        self.copy_gx(u, 0).start()
        for off in range(1, self.l.na):
            self.copy_gz(u, off).start()
        self.copy_own(u).start()

    def step_on(self, u):
        for off in range(1, self.l.na):
            self.copy_gz(u, off).wait_recv()
            self.copy_gx(u, off).start()

    def finish(self, u):
        self.copy_y(u).wait_send()
        for i in range(self.l.na):
            self.copy_x(u, i).wait_send()
        for off in range(1, self.l.na):
            self.copy_z(u, off).wait_send()
            self.copy_gz(u, off).wait_send()
        for off in range(self.l.na):
            self.copy_gx(u, off).wait()
        self.copy_own(u).wait()


def reducer_scratch(ndp, rows, cols, units=UNITS):
    bf = jnp.bfloat16
    na = ndp // 2
    cr, cc = chunk_rows(ndp, rows), cols
    dma = pltpu.SemaphoreType.DMA
    bufs = [
        pltpu.VMEM((units, cr * ndp, cols), bf),
        pltpu.VMEM((units, rows, cols), bf),
        pltpu.VMEM((units, rows, cols), bf),
        pltpu.VMEM((units, na, cr, cc), bf),
        pltpu.VMEM((units, na - 1, cr, cc), bf),
        pltpu.VMEM((units, cr, cc), bf),
    ]
    shapes = {"y": (units,), "x": (units, na), "z": (units, na - 1), "gz": (units, na - 1), "gx": (units, na)}
    sems = []
    for shape in shapes.values():
        sems += [dma(shape), dma(shape)]
    sems.append(dma((units,)))
    return bufs, sems, list(shapes)


class SmallSum:
    def __init__(self, links, mine, got, column, sems):
        self.l, self.mine, self.got, self.col = links, mine, got, column
        self.ss, self.rs = sems

    def swap(self, i):
        to = (self.l.core, self.l.far, self.l.pair)[i]
        return remote(self.mine.at[i], self.got.at[i], self.ss.at[i], self.rs.at[i], to)

    def spread(self, off):
        at = self.col.at[self.l.a]
        i = 2 + off
        return remote(at, at, self.ss.at[i], self.rs.at[i], self.l.column(off))

    def start(self, i):
        self.swap(i).start()

    def add(self, i):
        self.swap(i).wait_recv()
        total = self.mine[i] + self.got[i]
        if i < 2:
            self.mine[i + 1] = total
            self.start(i + 1)
        else:
            self.col[pl.ds(self.l.a, 1)] = total[None]
            for off in range(1, self.l.na):
                self.spread(off).start()

    def result(self):
        for off in range(1, self.l.na):
            self.spread(off).wait_recv()
        total = self.col[0]
        for i in range(1, self.l.na):
            total = total + self.col[i]
        return total

    def finish(self):
        for i in range(3):
            self.swap(i).wait_send()
        for off in range(1, self.l.na):
            self.spread(off).wait_send()


def small_scratch(ndp, rows, cols):
    f32 = jnp.float32
    na = ndp // 2
    dma = pltpu.SemaphoreType.DMA
    return [
        pltpu.VMEM((3, rows, cols), f32),
        pltpu.VMEM((3, rows, cols), f32),
        pltpu.VMEM((na, rows, cols), f32),
        dma((2 + na,)),
        dma((2 + na,)),
    ]


def reduce_kernel(ndp, rows, cols, parts, small_in, fin, small_out, *scratch):
    near, far, ybuf, xbuf, zbuf, own, cbuf = scratch[:7]
    names = ["y", "x", "z", "gz", "gx"]
    sems = {n: (scratch[7 + 2 * i], scratch[8 + 2 * i]) for i, n in enumerate(names)}
    sems["own"] = scratch[17]
    cs, cr, ld = scratch[18:21]
    sm = scratch[21:]
    l = Links(ndp)
    red = Reducer(l, (near, far, ybuf, xbuf, zbuf, own, fin), sems, rows, cols)
    small = SmallSum(l, sm[0], sm[1], sm[2], sm[3:5])
    f32 = jnp.float32

    def ccopy(u, i):
        return remote(parts.at[2 * i + 1, u], cbuf.at[u, i], cs.at[u, i], cr.at[u, i], l.core)

    def load(u, i):
        to = (near, far)[i].at[u, pl.ds(0, rows)]
        return pltpu.make_async_copy(parts.at[2 * i, u], to, ld.at[u, i])

    small.mine[0] = small_in[...]
    red.clear_padding()
    for u in range(UNITS):
        for i in (1, 0):
            load(u, i).start()
    l.greet()
    for u in range(UNITS):
        for i in (1, 0):
            ccopy(u, i).start()
    small.start(0)

    def merge(u, i):
        ref = (near, far)[i]
        load(u, i).wait()
        ccopy(u, i).wait_recv()
        total = ref[u, :rows].astype(f32) + cbuf[u, i].astype(f32)
        ref[u, :rows] = total.astype(ref.dtype)

    for u in range(UNITS):
        merge(u, 1)
        if u < WINDOW:
            red.start_y(u)
    for u in range(UNITS):
        merge(u, 0)
    for i in range(3):
        small.add(i)
    small_out[...] = small.result()
    for u in range(UNITS + 1):
        if u < UNITS:
            red.step_x(u)
        if u >= 1:
            red.step_own(u - 1)
        if u < UNITS:
            red.step_z(u)
        if u >= 1:
            red.step_on(u - 1)
    for u in range(UNITS):
        red.finish(u)
        for i in range(2):
            ccopy(u, i).wait_send()
    small.finish()


def reduce_gradients(ndp, parts, small):
    _, units, rows, cols = parts.shape
    bufs, sems, _ = reducer_scratch(ndp, rows, cols)
    dma = pltpu.SemaphoreType.DMA
    bf = jnp.bfloat16
    return pl.pallas_call(
        partial(reduce_kernel, ndp, rows, cols),
        in_specs=[pl.BlockSpec(memory_space=pl.ANY), pl.BlockSpec(memory_space=pltpu.VMEM)],
        out_specs=[pl.BlockSpec(memory_space=pl.ANY), pl.BlockSpec(memory_space=pltpu.VMEM)],
        out_shape=[
            jax.ShapeDtypeStruct((units, chunk_rows(ndp, rows) * ndp, cols), bf),
            jax.ShapeDtypeStruct(small.shape, jnp.float32),
        ],
        scratch_shapes=[
            *bufs,
            pltpu.VMEM((units, 2, rows, cols), bf),
            *sems,
            dma((units, 2)),
            dma((units, 2)),
            dma((units, 2)),
            *small_scratch(ndp, *small.shape),
        ],
        compiler_params=pltpu.CompilerParams(
            collective_id=1, has_side_effects=True, vmem_limit_bytes=VMEM_LIMIT
        ),
    )(parts, small)


def norm_forward(values):
    center = jnp.mean(values, axis=-1, keepdims=True)
    centered = values - center
    spread = jnp.mean(centered * centered, axis=-1, keepdims=True)
    scale = lax.rsqrt(spread + EPSILON)
    return centered * scale, scale


def norm_backward(grad, unit, scale, gain):
    n = grad * gain
    mean_n = jnp.mean(n, axis=-1, keepdims=True)
    mean_nx = jnp.mean(n * unit, axis=-1, keepdims=True)
    return scale * (n - mean_n - unit * mean_nx)


def gelu_parts(gate):
    cdf = 0.5 * (1.0 + lax.erf(gate * (0.5**0.5)))
    pdf = jnp.exp(-0.5 * gate * gate) * ((0.5 / jnp.pi) ** 0.5)
    return cdf, pdf


def per_device(
    tokens,
    type_ids,
    boundary,
    token_type_rows,
    query_key_value_weight,
    b_qv,
    output_weight,
    b_out,
    gain_one,
    shift_one,
    gate_up_weight,
    gate_up_bias,
    down_weight,
    b_down,
    gain_two,
    shift_two,
    cotangent,
):
    bf = jnp.bfloat16
    f32 = jnp.float32
    nt = lax.axis_size("tensor")
    ndp = lax.axis_size("dp")
    t = lax.axis_index("tensor")
    dp = lax.axis_index("dp")
    y = t // 2
    c = t % 2
    rows_dev = tokens.shape[1]
    width = tokens.shape[2]
    qcols = query_key_value_weight.shape[2]
    heads_dev = qcols // HEAD_DIM
    ff_dev = down_weight.shape[0]
    flip_y = [(i, i ^ 2) for i in range(nt)]
    flip_c = [(i, i ^ 1) for i in range(nt)]

    def over_y(a):
        return lax.ppermute(a, "tensor", flip_y)

    def over_c(a):
        return lax.ppermute(a, "tensor", flip_c)

    def pick(a, i):
        return lax.dynamic_index_in_dim(a, i, 0, keepdims=False)

    tok_other = over_y(pick(tokens, 1 - y))
    tok_rows = jnp.concatenate([pick(tokens, y), tok_other], axis=0)

    def gather_quarters(w):
        n = w.shape[0] // ndp
        if w.shape[0] % ndp:
            far = over_y(w)
            return w, over_c(w), far, over_c(far)
        part = over_y(lax.dynamic_slice_in_dim(w, dp * n, n, 0))
        far = lax.all_gather(part, "dp", axis=0, tiled=True)
        return w, over_c(w), far, over_c(far)

    w_qkv = gather_quarters(query_key_value_weight.reshape(width, 3 * qcols))
    w_out = gather_quarters(output_weight)
    w_gu = gather_quarters(gate_up_weight.reshape(width, 2 * ff_dev))
    w_down = gather_quarters(down_weight)
    cot_other = over_y(pick(cotangent, 1 - y))
    cot = jnp.concatenate([pick(cotangent, y), cot_other], axis=0).astype(f32)

    bqv_all = lax.all_gather(b_qv, "tensor", axis=0)
    bgu_all = lax.all_gather(gate_up_bias, "tensor", axis=0)
    bqv = [pick(bqv_all, t ^ s) for s in range(nt)]
    bgu = [pick(bgu_all, t ^ s) for s in range(nt)]

    pos_own = (2 * y + c) * rows_dev
    pos_far = (2 * (1 - y) + c) * rows_dev
    pos_own_p = (2 * y + 1 - c) * rows_dev
    pos_far_p = (2 * (1 - y) + 1 - c) * rows_dev
    bases = jnp.stack([pos_own, pos_far, pos_own_p, pos_far_p]).astype(jnp.int32)
    place = jnp.concatenate([pos_own + jnp.arange(rows_dev), pos_far + jnp.arange(rows_dev)])
    pair = pick(type_ids, y)
    bound = pick(boundary, y)
    kind = jnp.where(place >= bound, pair[1], pair[0])
    table0, table1 = token_type_rows[0], token_type_rows[1]
    entered = tok_rows.astype(f32) + jnp.where((kind == 1)[:, None], table1, table0)
    entered_low = entered.astype(bf)

    head_ids = jnp.concatenate(
        [(t ^ s) * heads_dev + jnp.arange(heads_dev) for s in range(nt)]
    )
    slopes = jnp.exp2(-8.0 * (head_ids + 1).astype(f32) / HEADS)

    qs, ks, vs = [], [], []
    for s in range(nt):
        bias = jnp.concatenate([bqv[s][0], jnp.zeros_like(bqv[s][0]), bqv[s][1]])
        part = (dot(entered_low, w_qkv[s]) + bias).astype(bf)
        qs.append(part[:, :qcols])
        ks.append(part[:, qcols : 2 * qcols])
        vs.append(part[:, 2 * qcols :])
    kv_send = jnp.concatenate([*(ks[s ^ 1] for s in range(nt)), *(vs[s ^ 1] for s in range(nt))], axis=1)
    kv_own = jnp.concatenate([*ks, *vs], axis=1)
    kv = jnp.concatenate([kv_own, over_c(kv_send)], axis=0)
    q = jnp.concatenate(qs, axis=1)
    k, v = kv[:, :width], kv[:, width:]
    context, lse = attention_forward(slopes, bases, q, k, v)
    w_out_full = jnp.concatenate(w_out, axis=0)
    attn = dot(context, w_out_full)
    unit_one, scale_one = norm_forward(attn + b_out + entered)
    h1 = unit_one * gain_one + shift_one
    h1_low = h1.astype(bf)
    gates, ups, hiddens = [], [], []
    ffn = 0.0
    for s in range(nt):
        gu = dot(h1_low, w_gu[s]) + bgu[s].reshape(-1)
        gate, up = gu[:, :ff_dev], gu[:, ff_dev:]
        cdf, _ = gelu_parts(gate)
        hidden = (gate * cdf * up).astype(bf)
        gates.append(gate)
        ups.append(up)
        hiddens.append(hidden)
        ffn = ffn + dot(hidden, w_down[s])
    unit_two, scale_two = norm_forward(ffn + b_down + h1)
    output = (unit_two * gain_two + shift_two).astype(bf)

    g_second = norm_backward(cot, unit_two, scale_two, gain_two)
    grad_gain_two = jnp.sum(cot * unit_two, axis=0)
    grad_shift_two = jnp.sum(cot, axis=0)
    grad_b_down = jnp.sum(g_second, axis=0)
    g_ffn = g_second.astype(bf)
    g_h1 = g_second
    grad_down, grad_gu, grad_bgu = [], [], []
    for s in range(nt):
        g_hidden = dot(g_ffn, w_down[s], NT)
        grad_down.append(dot(g_ffn, hiddens[s], TN).astype(bf))
        cdf, pdf = gelu_parts(gates[s])
        g_gate = g_hidden * ups[s] * (cdf + gates[s] * pdf)
        g_up = g_hidden * (gates[s] * cdf)
        g_gu = jnp.concatenate([g_gate, g_up], axis=1).astype(bf)
        grad_bgu.append(jnp.sum(g_gu.astype(f32), axis=0))
        grad_gu.append(dot(h1_low, g_gu, TN).astype(bf))
        g_h1 = g_h1 + dot(g_gu, w_gu[s], NT)
    g_mixed = norm_backward(g_h1, unit_one, scale_one, gain_one)
    grad_gain_one = jnp.sum(g_h1 * unit_one, axis=0)
    grad_shift_one = jnp.sum(g_h1, axis=0)
    grad_b_out = jnp.sum(g_mixed, axis=0)
    g_attn = g_mixed.astype(bf)
    grad_out_all = dot(g_attn, context, TN).astype(bf)
    grad_out = [grad_out_all[:, s * qcols : (s + 1) * qcols] for s in range(nt)]
    g_context = dot(g_attn, w_out_full, NT).astype(bf)
    dq, dk, dv = attention_backward(slopes, bases, q, k, v, g_context, lse)
    rows = q.shape[0]
    dkv_other = jnp.concatenate(
        [a[rows:, (s ^ 1) * qcols : ((s ^ 1) + 1) * qcols] for a in (dk, dv) for s in range(nt)], axis=1
    ).astype(bf)
    dkv = jnp.concatenate([dk[:rows], dv[:rows]], axis=1) + over_c(dkv_other).astype(f32)
    dkv = dkv.astype(bf)
    grad_qkv, grad_bqv = [], []
    g_entered = g_mixed
    for s in range(nt):
        cols = slice(s * qcols, (s + 1) * qcols)
        g_part = jnp.concatenate([dq[:, cols], dkv[:, :width][:, cols], dkv[:, width:][:, cols]], axis=1)
        grad_qkv.append(dot(entered_low, g_part, TN).astype(bf))
        sums = jnp.sum(g_part.astype(f32), axis=0)
        grad_bqv.append(jnp.stack([sums[:qcols], sums[2 * qcols :]]))
        g_entered = g_entered + dot(g_part, w_qkv[s], NT)
    second = (kind == 1).astype(f32)[:, None]
    sum_all = jnp.sum(g_entered, axis=0)
    sum_second = jnp.sum(g_entered * second, axis=0)
    grad_table = jnp.stack([sum_all - sum_second, sum_second])

    half = ff_dev // 2
    units = []
    for s in range(nt):
        mats = [grad_down[s], grad_gu[s][:, :ff_dev], grad_gu[s][:, ff_dev:], jnp.concatenate([grad_qkv[s], grad_out[s]], axis=1)]
        units.append(jnp.stack([m[:, i * half : (i + 1) * half] for m in mats for i in range(2)]))

    def by_quarter(parts):
        stacked = jnp.stack(parts)
        return jnp.stack([pick(stacked, t ^ s) for s in range(nt)])

    bq = by_quarter(grad_bqv)
    vectors = jnp.concatenate(
        [
            grad_table,
            jnp.stack([grad_b_out, grad_gain_one, grad_shift_one, grad_b_down, grad_gain_two, grad_shift_two]),
            by_quarter(grad_bgu).reshape(2 * nt, ff_dev),
            jnp.pad(bq.reshape(nt, 2 * qcols), ((0, 0), (0, width - 2 * qcols))),
        ],
        axis=0,
    )
    vectors = jnp.pad(vectors, ((0, -vectors.shape[0] % 8), (0, 0)))
    done, sums = reduce_gradients(ndp, jnp.stack(units), vectors)
    done = done[:, :width].astype(f32)
    full = [jnp.concatenate([done[2 * i], done[2 * i + 1]], axis=1) for i in range(4)]
    g_w_down = full[0].T
    g_w_gu = jnp.stack([full[1], full[2]], axis=1)
    g_w_qkv = full[3][:, : 3 * qcols].reshape(query_key_value_weight.shape)
    g_w_out = full[3][:, 3 * qcols :].T
    g_table = sums[:2]
    first = 8
    g_bgu = lax.dynamic_slice_in_dim(sums, first + 2 * t, 2, 0)
    g_bqv = pick(sums, first + 2 * nt + t)[: 2 * qcols].reshape(2, qcols)
    sums = [g_table, *(sums[i] for i in range(2, 8))]

    def back(rows_all):
        own = rows_all[:rows_dev]
        other = over_y(rows_all[rows_dev:].astype(bf)).astype(own.dtype)
        both = jnp.stack([own, other])
        return jnp.stack([pick(both, y), pick(both, 1 - y)])

    return (
        back(output),
        back(g_entered),
        sums[0],
        g_w_qkv,
        g_bqv,
        g_w_out,
        sums[1],
        sums[2],
        sums[3],
        g_w_gu,
        g_bgu,
        g_w_down,
        sums[4],
        sums[5],
        sums[6],
    )


def solution(mesh):
    in_specs = (
        P("dp", "tensor", None),
        P("dp", None),
        P("dp"),
        P(),
        P(None, None, "tensor"),
        P(None, "tensor"),
        P("tensor", None),
        P(),
        P(),
        P(),
        P(None, None, "tensor"),
        P(None, "tensor"),
        P("tensor", None),
        P(),
        P(),
        P(),
        P("dp", "tensor", None),
    )
    out_specs = (
        P("dp", "tensor", None),
        P("dp", "tensor", None),
        P(),
        P(None, None, "tensor"),
        P(None, "tensor"),
        P("tensor", None),
        P(),
        P(),
        P(),
        P(None, None, "tensor"),
        P(None, "tensor"),
        P("tensor", None),
        P(),
        P(),
        P(),
    )
    return jax.shard_map(
        per_device, mesh=mesh, in_specs=in_specs, out_specs=out_specs, check_vma=False
    )
```

time: 863 us -> 562 us (0.65)
  waiting for transfers between devices: 514 us -> 11.4 us
  Pallas kernels: 0 us -> 195 us
  matrix products: 142 us -> 85 us
  local copies, waits for them, and re-layouts: 47.7 us -> 90.2 us
  blocking collectives: 66 us -> 86.1 us
  other arithmetic: 66.8 us -> 54.6 us
  starting transfers between devices: 2.59 us -> 12.6 us
    psum x1 -> x0, waiting for transfers between devices: 237 us -> none  [per_device(): lax.psum((grad_w_qkv, grad_b_qv, grad_w_out, grad_w_gu, grad_b_gu, grad_w...]
    pallas_call x0 -> x3, Pallas kernels: none -> 195 us  [the longest x1 158 us: reduce_gradients(): pl.pallas_call(partial(reduce_kernel, ndp, rows, cols), in_specs=[pl.Bloc...]
    reduce_scatter x8 -> x0, waiting for transfers between devices: 185 us -> none  [the longest x2 66.1 us: per_device(): lax.psum_scatter(ffn_terms, 'tensor', scatter_dimension=1, tiled=True)]
    all_gather x8 -> x2, waiting for transfers between devices: 91.5 us -> 0.01 us  [gather_quarters(): far = lax.all_gather(part, 'dp', axis=0, tiled=True)]
    all_gather x0 -> x4, blocking collectives: none -> 86.1 us  [the longest x2 67.1 us: gather_quarters(): far = lax.all_gather(part, 'dp', axis=0, tiled=True)]
    psum x2 -> x0, blocking collectives: 66 us -> none  [the longest x1 43.4 us: per_device(): lax.psum((grad_table, grad_b_out, grad_gain_one, grad_shift_one, grad_b_d...]
    dot_general x36 -> x39, matrix products: 133 us -> 85 us  [dot(): return lax.dot_general(a, b, dims, preferred_element_type=jnp.float32)]
    reduce_sum x20 -> x13, other arithmetic: 26.4 us -> 11.1 us  [the longest x1 3.15 us: per_device(): grad_b_down = jnp.sum(g_second, axis=0)]
  transfers between devices with their start and end apart: 17 -> 20, of which waited for: 14 -> 2; matrix products, arithmetic and copies ran while one was open for 20% -> 19% of each run, Pallas kernels for 0% -> 3%
where the time goes in v1:
time: 562 us; the launch traced here: 552 us
  Pallas kernels  195 us (35%)
  local copies, waits for them, and re-layouts  90.2 us (16%)
  blocking collectives  86.1 us (15%)
  matrix products  85 us (15%)
  other arithmetic  54.6 us (10%)
  between operations  16.3 us (3%)
  starting transfers between devices  12.6 us (2%)
  waiting for transfers between devices  11.4 us (2%)
    pallas_call x1, Pallas kernels, reduce_gradients(): pl.pallas_call(partial(reduce_kernel, ndp, rows, cols), in_specs=[pl.Bloc...  158 us
    dot_general x39, matrix products, dot(): return lax.dot_general(a, b, dims, preferred_element_type=jnp.float32)  85 us
    all_gather x2, blocking collectives, gather_quarters(): far = lax.all_gather(part, 'dp', axis=0, tiled=True)  67.1 us
    unnamed x297, local copies, waits for them, and re-layouts  44.3 us
    pallas_call x1, Pallas kernels, attention_backward(): pl.pallas_call(attention_backward_kernel, grid=(pairs,), in_specs=[pl.Blo...  22.7 us
    pallas_call x1, Pallas kernels, attention_forward(): pl.pallas_call(attention_forward_kernel, grid=(pairs,), in_specs=[pl.Bloc...  14.6 us
    all_gather x1, blocking collectives, per_device(): bqv_all = lax.all_gather(b_qv, 'tensor', axis=0)  11.7 us
    ppermute x8, waiting for transfers between devices, over_y(): return lax.ppermute(a, 'tensor', flip_y)  11.3 us
  transfers between devices with their start and end apart: 20, of which 2 were waited for; matrix products, arithmetic and copies ran while one was open for 19% of the time, Pallas kernels for 3%

profile of v1, /device:TPU:0, one launch (start us, length us, event | category | flops | bytes accessed | tf_op | source)
XLA Modules:
  0.0 551.7 jit_solution(5108525682069339441)
XLA Ops:
  8.3 3.0 collective-permute-start.11
  11.4 3.8 collective-permute-done.11
  26.2 11.7 %all-gather.2 = f32[4,2,192]{2,1,0:T(2,128)S(1)} all-gather(f32[1,2,192]{2,1,0:T(2,128)S(1)} %bitcast.293), channel_id=2, replica_groups=mesh['dp'=8,'tensor'=4] {'tensor'}, dimensions={0}, use_global_device_ids=true | all-gather | bytes 7680 | tf_op jit(solution)/shard_map/all_gather | solution.py:564
  38.7 2.5 fusion.117
  41.4 34.9 %all_gather.26 = bf16[768,576]{1,0:T(8,128)(2,1)S(1)} all-gather(bf16[96,576]{1,0:T(8,128)(2,1)S(1)} %copy.88), channel_id=1, replica_groups=mesh['dp'=8,'tensor'=4] {'dp'}, dimensions={0}, use_global_device_ids=true | all-gather | bytes 995328 | tf_op jit(solution)/shard_map/all_gather | solution.py:554
  95.1 7.3 %all-gather.3 = f32[4,2,768]{2,1,0:T(2,128)S(1)} all-gather(f32[1,2,768]{2,1,0:T(2,128)S(1)} %bitcast.276), channel_id=3, replica_groups=mesh['dp'=8,'tensor'=4] {'tensor'}, dimensions={0}, use_global_device_ids=true | all-gather | bytes 30720 | tf_op jit(solution)/shard_map/all_gather | solution.py:565
  105.2 32.2 %all_gather.27 = bf16[192,768]{1,0:T(8,128)(2,1)S(1)} all-gather(bf16[24,768]{1,0:T(8,128)(2,1)} %collective-permute-done.6), channel_id=1, replica_groups=mesh['dp'=8,'tensor'=4] {'dp'}, dimensions={0}, use_global_device_ids=true | all-gather | bytes 331776 | tf_op jit(solution)/shard_map/all_gather | solution.py:554
  149.3 3.2 pad_maximum_fusion.3
  152.5 14.6 %shard_map.280 = (bf16[512,768]{1,0:T(8,128)(2,1)}, f32[6,2,512]{2,1,0:T(2,128)}) custom-call(f32[12]{0:T(128)} %fusion.92.slope_ref, s32[4]{0:T(128)} %pad_add_fusion.base_ref, bf16[512,768]{1,0:T(8,128)(2,1)} %pad_maximum_fusion.10.q_ref, bf16[1024,768]{1,0:T(8,128)(2,1)} %get-tuple-element.147.k_ref, bf16[1024,768]{1,0:T(8,128)(2,1)} %get-tuple-element.146.v_ref), custom_call_target="tpu_custom_call" | custom-call | flops 6442450944 | bytes 9437184 | tf_op jit(solution)/shard_map/pallas_call | solution.py:69
  170.4 5.0 convolution_add_fusion.2
  177.9 3.3 convolution_add_fusion.3
  191.3 2.5 fusion.118
  196.9 3.2 fusion.114
  201.6 3.7 fusion.80
  205.3 2.5 fusion.19
  209.2 3.1 fusion.31
  212.2 3.1 fusion.79
  216.8 2.6 multiply_reduce_fusion
  222.4 22.7 %shard_map.281 = (bf16[512,768]{1,0:T(8,128)(2,1)}, f32[1024,768]{1,0:T(8,128)}, f32[1024,768]{1,0:T(8,128)}) custom-call(f32[12]{0:T(128)} %fusion.92.slope_ref, s32[4]{0:T(128)} %pad_add_fusion.base_ref, bf16[512,768]{1,0:T(8,128)(2,1)} %pad_maximum_fusion.10.q_ref, bf16[1024,768]{1,0:T(8,128)(2,1)} %get-tuple-element.147.k_ref, ...), custom_call_target="tpu_custom_call" | custom-call | flops 16106127360 | bytes 18874368 | tf_op jit(solution)/shard_map/pallas_call | solution.py:138
  257.9 2.8 convolution_convert_fusion.3
  262.6 2.8 convolution_convert_fusion.2
  267.4 2.8 convolution_convert_fusion.1
  270.2 2.8 convolution_convert_fusion
  276.0 4.0 concatenate.126
  302.0 7.5 %collective-permute-done.14 = bf16[256,768]{1,0:T(8,128)(2,1)} collective-permute-done((bf16[256,768]{1,0:T(8,128)(2,1)}, bf16[256,768]{1,0:T(8,128)(2,1)}, u32[]{:S(2)}, u32[]{:S(2)}) %collective-permute-start.14) | collective-permute-done | bytes 393248 | tf_op jit(solution)/shard_map/ppermute | solution.py:537
  322.6 2.8 fusion.113
  337.1 2.4 convolution_convert_fusion.9
  341.4 10.7 %pad_maximum_fusion.parts = bf16[4,8,768,384]{3,2,1,0:T(8,128)(2,1)} fusion(bf16[1,8,768,384]{3,2,1,0:T(8,128)(2,1)} %bitcast.61, bf16[1,8,768,384]{3,2,1,0:T(8,128)(2,1)S(1)} %bitcast.269, bf16[1,8,768,384]{3,2,1,0:T(8,128)(2,1)S(1)} %bitcast.266, bf16[1,8,768,384]{3,2,1,0:T(8,128)(2,1)S(1)} %bitcast.263), kind=kLoop, calls=%fused_computation | loop fusion | flops 28311552 | bytes 37748736 | tf_op jit(solution)/shard_map/stack | solution.py:686
  352.2 158.2 %shard_map.282 = (bf16[8,768,384]{2,1,0:T(8,128)(2,1)}, f32[24,768]{1,0:T(8,128)}) custom-call(bf16[4,8,768,384]{3,2,1,0:T(8,128)(2,1)} %pad_maximum_fusion.parts, f32[24,768]{1,0:T(8,128)} %pad.9.small_in), custom_call_target="tpu_custom_call" | custom-call | tf_op jit(solution)/shard_map/pallas_call | solution.py:457
  510.3 3.0 convert_element_type.182
  519.0 2.5 pad_maximum_fusion.1
  526.5 8.3 %copy.99 = f32[768,2,768]{2,1,0:T(2,128)} copy(f32[768,2,768]{2,0,1:T(8,128)} %pad_maximum_fusion.1) | data formatting | bytes 9437184
  (486 shorter events, 159.7 us)
Async XLA Ops:
  7.2 30.8 %copy-start = (s32[2,2]{1,0:T(2,128)S(1)}, s32[2,2]{1,0:T(2,128)}, u32[]{:S(2)}) copy-start(s32[2,2]{1,0:T(2,128)} %param.18) | copy-start | bytes 52
  7.2 141.8 %all-gather.9.cloned.1.call-start = ((), (), s32[]{:S(2)}) async-start(), calls=%async_computation.1 | async-start | bytes 1327104 | tf_op jit(solution)/shard_map/all_gather | solution.py:554
  8.3 6.9 %collective-permute-start.11 = (bf16[96,768]{1,0:T(8,128)(2,1)S(1)}, bf16[96,768]{1,0:T(8,128)(2,1)S(1)}, u32[]{:S(2)}, u32[]{:S(2)}) collective-permute-start(bf16[96,768]{1,0:T(8,128)(2,1)S(1)} %constant_dynamic-slice_fusion.15), channel_id=1, source_target_pairs={{0,2},{1,3},{2,0},{3,1},{4,6},{5,7},{6,4},{7,5},{8,10},{9,11},{10,... | collective-permute-start | bytes 442376 | tf_op jit(solution)/shard_map/ppermute | solution.py:537
  15.9 159.5 %all-gather.7.cloned.1.call-start = ((), (), s32[]{:S(2)}) async-start(), calls=%async_computation | async-start | bytes 2654208 | tf_op jit(solution)/shard_map/all_gather | solution.py:554
  17.2 66.7 %copy-start.82 = (bf16[256,768]{1,0:T(8,128)(2,1)}, bf16[256,768]{1,0:T(8,128)(2,1)S(1)}, u32[]{:S(2)}) copy-start(bf16[256,768]{1,0:T(8,128)(2,1)S(1)} %get-tuple-element.181) | copy-start | bytes 1179652
  17.2 61.1 %collective-permute-start = (bf16[256,768]{1,0:T(8,128)(2,1)S(1)}, bf16[256,768]{1,0:T(8,128)(2,1)}, u32[]{:S(2)}, u32[]{:S(2)}) collective-permute-start(bf16[256,768]{1,0:T(8,128)(2,1)S(1)} %get-tuple-element.182), channel_id=1, source_target_pairs={{0,2},{1,3},{2,0},{3,1},{4,6},{5,7},{6,4},{7,5},{8,10},{9,11},{10,... | collective-permute-start | bytes 1179656 | tf_op jit(solution)/shard_map/ppermute | solution.py:537
  19.0 64.9 %collective-permute-start.1 = (bf16[768,576]{0,1:T(8,128)(2,1)}, bf16[768,576]{0,1:T(8,128)(2,1)}, u32[]{:S(2)}, u32[]{:S(2)}) collective-permute-start(bf16[768,576]{0,1:T(8,128)(2,1)} %bitcast.272), channel_id=1, source_target_pairs={{0,1},{1,0},{2,3},{3,2},{4,5},{5,4},{6,7},{7,6},{8,9},{9,8},{10,11... | collective-permute-start | bytes 2654216 | tf_op jit(solution)/shard_map/ppermute | solution.py:540
  20.7 20.5 %collective-permute-start.2 = (bf16[96,576]{0,1:T(8,128)(2,1)}, bf16[96,576]{0,1:T(8,128)(2,1)S(1)}, u32[]{:S(2)}, u32[]{:S(2)}) collective-permute-start(bf16[96,576]{0,1:T(8,128)(2,1)} %constant_dynamic-slice_fusion.23), channel_id=1, source_target_pairs={{0,2},{1,3},{2,0},{3,1},{4,6},{5,7},{6,4},{7,5},{8,10},{9,11},{10,... | collective-permute-start | bytes 331784 | tf_op jit(solution)/shard_map/ppermute | solution.py:537
  21.0 17.7 %copy-start.109 = (f32[2,768]{1,0:T(2,128)S(1)}, f32[2,768]{1,0:T(2,128)}, u32[]{:S(2)}) copy-start(f32[2,768]{1,0:T(2,128)} %param.20) | copy-start | bytes 18436
  23.8 53.7 %collective-permute-start.10 = (bf16[96,1536]{1,0:T(8,128)(2,1)S(1)}, bf16[96,1536]{1,0:T(8,128)(2,1)S(1)}, u32[]{:S(2)}, u32[]{:S(2)}) collective-permute-start(bf16[96,1536]{1,0:T(8,128)(2,1)S(1)} %constant_dynamic-slice_fusion.17), channel_id=1, source_target_pairs={{0,2},{1,3},{2,0},{3,1},{4,6},{5,7},{6,4},{7,5},{8,10},{9,11},{10,... | collective-permute-start | bytes 884744 | tf_op jit(solution)/shard_map/ppermute | solution.py:537
  38.7 128.4 %copy-start.112 = (f32[768]{0:T(1024)}, f32[768]{0:T(1024)S(1)}, u32[]{:S(2)}) copy-start(f32[768]{0:T(1024)S(1)} %get-tuple-element.120) | copy-start | bytes 9220
  38.7 128.4 %copy-start.114 = (f32[768]{0:T(1024)}, f32[768]{0:T(1024)S(1)}, u32[]{:S(2)}) copy-start(f32[768]{0:T(1024)S(1)} %get-tuple-element.121) | copy-start | bytes 9220
  41.2 45.6 %copy-start.118 = (pred[512]{0:T(512)(128)(4,1)}, pred[512]{0:T(512)(128)(4,1)S(1)}, u32[]{:S(2)}) copy-start(pred[512]{0:T(512)(128)(4,1)S(1)} %get-tuple-element.127) | copy-start | bytes 1540
  77.5 9.3 %collective-permute-start.3 = (bf16[768,576]{0,1:T(8,128)(2,1)}, bf16[768,576]{0,1:T(8,128)(2,1)}, u32[]{:S(2)}, u32[]{:S(2)}) collective-permute-start(bf16[768,576]{0,1:T(8,128)(2,1)} %copy.90), channel_id=1, source_target_pairs={{0,1},{1,0},{2,3},{3,2},{4,5},{5,4},{6,7},{7,6},{8,9},{9,8},{10,11... | collective-permute-start | bytes 2654216 | tf_op jit(solution)/shard_map/ppermute | solution.py:540
  92.3 57.0 %collective-permute-start.4 = (bf16[512,1536]{1,0:T(8,128)(2,1)}, bf16[512,1536]{1,0:T(8,128)(2,1)}, u32[]{:S(2)}, u32[]{:S(2)}) collective-permute-start(bf16[512,1536]{1,0:T(8,128)(2,1)} %concatenate.117), channel_id=1, source_target_pairs={{0,1},{1,0},{2,3},{3,2},{4,5},{5,4},{6,7},{7,6},{8,9},{9,8},{10,11... | collective-permute-start | bytes 4718600 | tf_op jit(solution)/shard_map/ppermute | solution.py:540
  92.8 77.5 %collective-permute-start.8 = (bf16[768,1536]{1,0:T(8,128)(2,1)}, bf16[768,1536]{1,0:T(8,128)(2,1)}, u32[]{:S(2)}, u32[]{:S(2)}) collective-permute-start(bf16[768,1536]{1,0:T(8,128)(2,1)} %bitcast.89), channel_id=1, source_target_pairs={{0,1},{1,0},{2,3},{3,2},{4,5},{5,4},{6,7},{7,6},{8,9},{9,8},{10,11... | collective-permute-start | bytes 7077896 | tf_op jit(solution)/shard_map/ppermute | solution.py:540
  92.9 90.5 %collective-permute-start.9 = (bf16[768,768]{1,0:T(8,128)(2,1)}, bf16[768,768]{1,0:T(8,128)(2,1)}, u32[]{:S(2)}, u32[]{:S(2)}) collective-permute-start(bf16[768,768]{1,0:T(8,128)(2,1)} %param.29), channel_id=1, source_target_pairs={{0,1},{1,0},{2,3},{3,2},{4,5},{5,4},{6,7},{7,6},{8,9},{9,8},{10,11... | collective-permute-start | bytes 3538952 | tf_op jit(solution)/shard_map/ppermute | solution.py:540
  93.4 47.1 %collective-permute-start.5 = (bf16[192,768]{1,0:T(8,128)(2,1)S(1)}, bf16[192,768]{1,0:T(8,128)(2,1)S(1)}, u32[]{:S(2)}, u32[]{:S(2)}) collective-permute-start(bf16[192,768]{1,0:T(8,128)(2,1)S(1)} %copy-done.86), channel_id=1, source_target_pairs={{0,1},{1,0},{2,3},{3,2},{4,5},{5,4},{6,7},{7,6},{8,9},{9,8},{10,11... | collective-permute-start | bytes 884744 | tf_op jit(solution)/shard_map/ppermute | solution.py:540
  93.4 11.7 %collective-permute-start.6 = (bf16[24,768]{1,0:T(8,128)(2,1)S(1)}, bf16[24,768]{1,0:T(8,128)(2,1)}, u32[]{:S(2)}, u32[]{:S(2)}) collective-permute-start(bf16[24,768]{1,0:T(8,128)(2,1)S(1)} %constant_dynamic-slice_fusion.20), channel_id=1, source_target_pairs={{0,2},{1,3},{2,0},{3,1},{4,6},{5,7},{6,4},{7,5},{8,10},{9,11},{10,... | collective-permute-start | bytes 110600 | tf_op jit(solution)/shard_map/ppermute | solution.py:537
  103.0 35.0 %copy-start.94 = (f32[1,2,768]{2,1,0:T(2,128)S(1)}, f32[1,2,768]{2,1,0:T(2,128)}, u32[]{:S(2)}) copy-start(f32[1,2,768]{2,1,0:T(2,128)} %get-tuple-element.201) | copy-start | bytes 18436
  103.0 35.6 %copy-start.93 = (f32[1,2,768]{2,1,0:T(2,128)S(1)}, f32[1,2,768]{2,1,0:T(2,128)}, u32[]{:S(2)}) copy-start(f32[1,2,768]{2,1,0:T(2,128)} %get-tuple-element.202) | copy-start | bytes 18436
  103.0 36.2 %copy-start.92 = (f32[1,2,768]{2,1,0:T(2,128)S(1)}, f32[1,2,768]{2,1,0:T(2,128)}, u32[]{:S(2)}) copy-start(f32[1,2,768]{2,1,0:T(2,128)} %get-tuple-element.204) | copy-start | bytes 18436
  137.4 6.1 %collective-permute-start.7 = (bf16[192,768]{1,0:T(8,128)(2,1)S(1)}, bf16[192,768]{1,0:T(8,128)(2,1)S(1)}, u32[]{:S(2)}, u32[]{:S(2)}) collective-permute-start(bf16[192,768]{1,0:T(8,128)(2,1)S(1)} %all_gather.27), channel_id=1, source_target_pairs={{0,1},{1,0},{2,3},{3,2},{4,5},{5,4},{6,7},{7,6},{8,9},{9,8},{10,11... | collective-permute-start | bytes 884744 | tf_op jit(solution)/shard_map/ppermute | solution.py:540
  140.4 53.7 %collective-permute-start.15 = (bf16[256,768]{1,0:T(8,128)(2,1)}, bf16[256,768]{1,0:T(8,128)(2,1)}, u32[]{:S(2)}, u32[]{:S(2)}) collective-permute-start(bf16[256,768]{1,0:T(8,128)(2,1)} %get-tuple-element.176), channel_id=1, source_target_pairs={{0,2},{1,3},{2,0},{3,1},{4,6},{5,7},{6,4},{7,5},{8,10},{9,11},{10,... | collective-permute-start | bytes 1179656 | tf_op jit(solution)/shard_map/ppermute | solution.py:537
  149.0 42.1 %collective-permute-start.13 = (bf16[768,768]{1,0:T(8,128)(2,1)}, bf16[768,768]{1,0:T(8,128)(2,1)}, u32[]{:S(2)}, u32[]{:S(2)}) collective-permute-start(bf16[768,768]{1,0:T(8,128)(2,1)} %all-gather.9.cloned.1.call-done), channel_id=1, source_target_pairs={{0,1},{1,0},{2,3},{3,2},{4,5},{5,4},{6,7},{7,6},{8,9},{9,8},{10,11... | collective-permute-start | bytes 3538952 | tf_op jit(solution)/shard_map/ppermute | solution.py:540
  170.4 18.9 %copy-start.72 = (bf16[512,768]{1,0:T(8,128)(2,1)}, bf16[512,768]{1,0:T(8,128)(2,1)S(1)}, u32[]{:S(2)}) copy-start(bf16[512,768]{1,0:T(8,128)(2,1)S(1)} %fusion.34) | copy-start | bytes 2359300
  175.4 13.9 %collective-permute-start.12 = (bf16[768,1536]{1,0:T(8,128)(2,1)}, bf16[768,1536]{1,0:T(8,128)(2,1)S(1)}, u32[]{:S(2)}, u32[]{:S(2)}) collective-permute-start(bf16[768,1536]{1,0:T(8,128)(2,1)} %all-gather.7.cloned.1.call-done), channel_id=1, source_target_pairs={{0,1},{1,0},{2,3},{3,2},{4,5},{5,4},{6,7},{7,6},{8,9},{9,8},{10,11... | collective-permute-start | bytes 7077896 | tf_op jit(solution)/shard_map/ppermute | solution.py:540
  280.0 31.9 %collective-permute-start.16 = (bf16[512,1536]{1,0:T(8,128)(2,1)}, bf16[512,1536]{1,0:T(8,128)(2,1)}, u32[]{:S(2)}, u32[]{:S(2)}) collective-permute-start(bf16[512,1536]{1,0:T(8,128)(2,1)} %concatenate.126), channel_id=1, source_target_pairs={{0,1},{1,0},{2,3},{3,2},{4,5},{5,4},{6,7},{7,6},{8,9},{9,8},{10,11... | collective-permute-start | bytes 4718600 | tf_op jit(solution)/shard_map/ppermute | solution.py:540
  297.8 11.7 %collective-permute-start.14 = (bf16[256,768]{1,0:T(8,128)(2,1)}, bf16[256,768]{1,0:T(8,128)(2,1)}, u32[]{:S(2)}, u32[]{:S(2)}) collective-permute-start(bf16[256,768]{1,0:T(8,128)(2,1)} %get-tuple-element.179), channel_id=1, source_target_pairs={{0,2},{1,3},{2,0},{3,1},{4,6},{5,7},{6,4},{7,5},{8,10},{9,11},{10,... | collective-permute-start | bytes 1179656 | tf_op jit(solution)/shard_map/ppermute | solution.py:537
  299.5 20.1 %copy-start.31 = (bf16[512,192]{1,0:T(8,128)(2,1)}, bf16[512,192]{1,0:T(8,128)(2,1)S(1)}, u32[]{:S(2)}) copy-start(bf16[512,192]{1,0:T(8,128)(2,1)S(1)} %get-tuple-element.171) | copy-start | bytes 589828
  325.4 191.2 %copy-start.10 = (f32[512,768]{1,0:T(8,128)}, f32[512,768]{1,0:T(8,128)S(1)}, u32[]{:S(2)}) copy-start(f32[512,768]{1,0:T(8,128)S(1)} %get-tuple-element.234) | copy-start | bytes 4718596
  517.4 24.4 %collective-permute-start.17 = (bf16[256,768]{1,0:T(8,128)(2,1)}, bf16[256,768]{1,0:T(8,128)(2,1)}, u32[]{:S(2)}, u32[]{:S(2)}) collective-permute-start(bf16[256,768]{1,0:T(8,128)(2,1)} %slice.801), channel_id=1, source_target_pairs={{0,2},{1,3},{2,0},{3,1},{4,6},{5,7},{6,4},{7,5},{8,10},{9,11},{10,... | collective-permute-start | bytes 1179656 | tf_op jit(solution)/shard_map/ppermute | solution.py:537
  (119 other events, 394.9 us)
Sparse Core Ops, SparseCore 0:
  16.0 54.1 all-gather.8
  78.4 56.4 all-gather.6

commit v2 on v0

v2 whole, which is shorter than its diff:
```python
from functools import partial

import jax
import jax.numpy as jnp
from jax import lax
from jax.experimental import pallas as pl
from jax.experimental.pallas import tpu as pltpu
from jax.sharding import PartitionSpec as P

HEADS = 12
HEAD_DIM = 64
EPSILON = 1e-05
VMEM_LIMIT = 127 * 2**19
MESH = pl.DeviceIdType.MESH
BF = jnp.bfloat16
F32 = jnp.float32
NT = (((1,), (1,)), ((), ()))
TN = (((0,), (0,)), ((), ()))
NN = (((1,), (0,)), ((), ()))
DIRECT = (3,)


def dot(a, b, dims=NN):
    return lax.dot_general(a, b, dims, preferred_element_type=F32)


def remote(src, dst, send, recv, to):
    return pltpu.make_async_remote_copy(
        src_ref=src, dst_ref=dst, send_sem=send, recv_sem=recv, device_id=to, device_id_type=MESH
    )


def local(src, dst, sem):
    return pltpu.make_async_copy(src, dst, sem)


def dma(*shape):
    return pltpu.SemaphoreType.DMA(shape)


def chunk_rows(ndp, rows):
    return -(-rows // (16 * ndp)) * 16


class Links:
    def __init__(self, ndp):
        self.ndp = ndp
        self.na = ndp // 2
        self.dp = lax.axis_index("dp")
        self.t = lax.axis_index("tensor")
        self.a = self.dp // 2
        self.b = lax.rem(self.dp, 2)
        self.y = self.t // 2
        self.c = lax.rem(self.t, 2)
        self.core = (self.dp, 2 * self.y + 1 - self.c)
        self.far = (self.dp, 2 * (1 - self.y) + self.c)
        self.cross = (self.dp, 2 * (1 - self.y) + 1 - self.c)
        self.pair = (2 * self.a + 1 - self.b, self.t)

    def up(self, off):
        return lax.rem(self.a + off, self.na)

    def down(self, off):
        return lax.rem(self.a + self.na - off, self.na)

    def column(self, off):
        return (2 * self.up(off) + self.b, self.t)

    def quarter(self, s):
        return 2 * lax.rem(self.y + s // 2, 2) + lax.rem(self.c + s % 2, 2)

    def greet(self):
        barrier = pltpu.get_barrier_semaphore()
        others = [self.core, self.far, self.cross, self.pair]
        others += [self.column(o) for o in range(1, self.na)]
        for other in others:
            pl.semaphore_signal(barrier, inc=1, device_id=other, device_id_type=MESH)
        pl.semaphore_wait(barrier, len(others))


class Gather:
    def __init__(self, links, own, place, sems, rows):
        self.l, self.own, self.place, self.s = links, own, place, sems
        self.cr = rows // links.ndp
        self.fits = rows % (16 * links.ndp) == 0

    def relayed(self, m):
        return self.fits and m not in DIRECT

    def share(self, ref, d):
        return ref.at[pl.ds(pl.multiple_of(d * self.cr, 16), self.cr)]

    def pair_of(self, name, m, i=None):
        s, r = self.s[name]
        return (s.at[m], r.at[m]) if i is None else (s.at[m, i], r.at[m, i])

    def core(self, m):
        return remote(self.own.at[m], self.place(m, 1), *self.pair_of("c", m), self.l.core)

    def core_far(self, m):
        return remote(self.place(m, 2), self.place(m, 3), *self.pair_of("cf", m), self.l.core)

    def over_y(self, m):
        src, dst = self.own.at[m], self.place(m, 2)
        if self.relayed(m):
            src, dst = self.share(src, self.l.dp), self.share(dst, self.l.dp)
        return remote(src, dst, *self.pair_of("y", m), self.l.far)

    def over_x(self, m, off):
        at = self.share(self.place(m, 2), 2 * self.l.down(off) + self.l.b)
        return remote(at, at, *self.pair_of("x", m, off), self.l.pair)

    def over_z(self, m, off):
        at = self.share(self.place(m, 2), self.l.dp)
        return remote(at, at, *self.pair_of("z", m, off - 1), self.l.column(off))

    def step_spread(self, m):
        if self.relayed(m):
            self.over_y(m).wait_recv()
            self.over_x(m, 0).start()
            for off in range(1, self.l.na):
                self.over_z(m, off).start()

    def step_on(self, m):
        if self.relayed(m):
            for off in range(1, self.l.na):
                self.over_z(m, off).wait_recv()
                self.over_x(m, off).start()

    def step_core(self, m):
        if self.relayed(m):
            for off in range(self.l.na):
                self.over_x(m, off).wait_recv()
        else:
            self.over_y(m).wait_recv()
        self.core_far(m).start()

    def finish(self, m):
        self.core(m).wait_send()
        self.over_y(m).wait_send()
        self.core_far(m).wait_send()
        if self.relayed(m):
            for off in range(self.l.na):
                self.over_x(m, off).wait_send()
            for off in range(1, self.l.na):
                self.over_z(m, off).wait_send()


class Reducer:
    def __init__(self, links, refs, sems, rows, split):
        self.l = links
        self.near, self.far, self.ybuf, self.xbuf, self.zbuf, self.own, self.fin = refs
        self.s = sems
        self.split = split
        self.rows = rows // split
        self.cr = chunk_rows(links.ndp, self.rows)
        self.units = refs[3].shape[0]

    def clear_padding(self):
        used = self.rows * self.split
        if self.cr * self.l.ndp > self.rows:
            self.near[:, used:, :] = jnp.zeros_like(self.near[:, used:, :])

    def block(self, u):
        return u // self.split, u % self.split * self.rows

    def unit(self, ref, u):
        k, first = self.block(u)
        return ref.at[k, pl.ds(first, self.rows)]

    def at(self, ref, u, d):
        k, first = self.block(u)
        return ref.at[k, pl.ds(pl.multiple_of(first + d * self.cr, 16), self.cr)]

    def copy_y(self, u):
        s, r = self.s["y"]
        return remote(self.unit(self.far, u), self.unit(self.ybuf, u), s.at[u], r.at[u], self.l.far)

    def copy_x(self, u, i):
        s, r = self.s["x"]
        src = self.at(self.near, u, 2 * i + 1 - self.l.b)
        return remote(src, self.xbuf.at[u, i], s.at[u, i], r.at[u, i], self.l.pair)

    def copy_z(self, u, off):
        s, r = self.s["z"]
        src = self.at(self.near, u, 2 * self.l.up(off) + self.l.b)
        return remote(src, self.zbuf.at[u, off - 1], s.at[u, off - 1], r.at[u, off - 1], self.l.column(off))

    def copy_gz(self, u, off):
        s, r = self.s["gz"]
        dst = self.at(self.fin, u, self.l.dp)
        return remote(self.own.at[u], dst, s.at[u, off - 1], r.at[u, off - 1], self.l.column(off))

    def copy_gx(self, u, off):
        s, r = self.s["gx"]
        if off == 0:
            src, dst = self.own.at[u], self.at(self.fin, u, self.l.dp)
        else:
            src = dst = self.at(self.fin, u, 2 * self.l.down(off) + self.l.b)
        return remote(src, dst, s.at[u, off], r.at[u, off], self.l.pair)

    def copy_own(self, u):
        return local(self.own.at[u], self.at(self.fin, u, self.l.dp), self.s["own"].at[u])

    def start_y(self, u):
        if u < self.units:
            self.copy_y(u).start()

    def step_x(self, u):
        self.copy_y(u).wait_recv()
        ref = self.unit(self.near, u)
        ref[...] = (ref[...].astype(F32) + self.unit(self.ybuf, u)[...].astype(F32)).astype(BF)
        for i in range(self.l.na):
            self.copy_x(u, i).start()

    def step_z(self, u):
        for i in range(self.l.na):
            self.copy_x(u, i).wait_recv()
        for i in range(self.l.na):
            ref = self.at(self.near, u, 2 * i + self.l.b)
            ref[...] = (ref[...].astype(F32) + self.xbuf[u, i].astype(F32)).astype(BF)
        for off in range(1, self.l.na):
            self.copy_z(u, off).start()

    def step_own(self, u):
        total = self.at(self.near, u, self.l.dp)[...].astype(F32)
        for off in range(1, self.l.na):
            self.copy_z(u, off).wait_recv()
            total = total + self.zbuf[u, off - 1].astype(F32)
        self.own[u] = total.astype(BF)
        self.copy_gx(u, 0).start()
        for off in range(1, self.l.na):
            self.copy_gz(u, off).start()
        self.copy_own(u).start()

    def step_on(self, u):
        for off in range(1, self.l.na):
            self.copy_gz(u, off).wait_recv()
            self.copy_gx(u, off).start()

    def finish(self, u):
        self.copy_y(u).wait_send()
        for i in range(self.l.na):
            self.copy_x(u, i).wait_send()
        for off in range(1, self.l.na):
            self.copy_z(u, off).wait_send()
            self.copy_gz(u, off).wait_send()
        for off in range(self.l.na):
            self.copy_gx(u, off).wait()
        self.copy_own(u).wait()


class SmallSum:
    def __init__(self, links, mine, got, sems):
        self.l, self.mine, self.got = links, mine, got
        self.ss, self.rs = sems
        self.levels = got.shape[0]

    def partner(self, i):
        if i < 3:
            return (self.l.core, self.l.far, self.l.pair)[i]
        step = 2 ** (i - 3)
        a = self.l.a + step - 2 * step * lax.rem(self.l.a // step, 2)
        return (2 * a + self.l.b, self.l.t)

    def swap(self, i):
        return remote(self.mine.at[i], self.got.at[i], self.ss.at[i], self.rs.at[i], self.partner(i))

    def start(self, i):
        self.swap(i).start()

    def add(self, i):
        self.swap(i).wait_recv()
        total = self.mine[i] + self.got[i]
        if i + 1 < self.levels:
            self.mine[i + 1] = total
            self.start(i + 1)
        return total

    def finish(self):
        for i in range(self.levels):
            self.swap(i).wait_send()


def positions(links, size):
    y, c = links.y, links.c
    return [(2 * y + c) * size, (2 * (1 - y) + c) * size, (2 * y + 1 - c) * size, (2 * (1 - y) + 1 - c) * size]


def fill_distance(firsts, size, dist_ref):
    for kb, key in enumerate(firsts):
        for qb, query in enumerate(firsts[:2]):
            row = lax.broadcasted_iota(jnp.int32, (size, size), 0) + key
            col = lax.broadcasted_iota(jnp.int32, (size, size), 1) + query
            dist_ref[kb * size : (kb + 1) * size, qb * size : (qb + 1) * size] = jnp.abs(row - col).astype(F32)


def second_segment(firsts, size, kind_ref, block):
    place = lax.broadcasted_iota(jnp.int32, (size, 1), 0) + firsts[block]
    return jnp.where(place >= kind_ref[2], kind_ref[1], kind_ref[0]) == 1


def mean(a):
    return jnp.mean(a, axis=-1, keepdims=True)


def norm_forward(values):
    centered = values - mean(values)
    scale = lax.rsqrt(mean(centered * centered) + EPSILON)
    return centered * scale, scale


def norm_backward(grad, unit, scale, gain):
    n = grad * gain
    return scale * (n - mean(n) - unit * mean(n * unit))


def gelu_parts(gate):
    e = jnp.exp(gate * gate * -0.5)
    t = 1.0 / (1.0 + jnp.abs(gate) * (0.3275911 * 0.5**0.5))
    poly = t * (
        0.5 * 0.254829592
        + t * (0.5 * -0.284496736 + t * (0.5 * 1.421413741 + t * (0.5 * -1.453152027 + t * (0.5 * 1.061405429))))
    )
    tail = poly * e
    return jnp.where(gate < 0, tail, 1.0 - tail), e * 0.3989422804014327


class Names:
    def __init__(self):
        self.names, self.shapes = [], []

    def add(self, name, shape):
        self.names.append(name)
        self.shapes.append(shape)

    def pair(self, name, *shape):
        self.add(name + "_s", dma(*shape))
        self.add(name + "_r", dma(*shape))


ANY = pl.BlockSpec(memory_space=pl.ANY)
VMEM = pl.BlockSpec(memory_space=pltpu.VMEM)
SMEM = pl.BlockSpec(memory_space=pltpu.SMEM)


class Refs:
    def __init__(self, names, refs):
        self.__dict__.update(zip(names, refs))

    def sems(self, name):
        return getattr(self, name + "_s"), getattr(self, name + "_r")


ENTER_IN = ["tokens", "w4", "bias", "table", "kinds", "slopes"]
ENTER_OUT = ["x", "qkv", "kvp", "ctx", "lse", "wall", "biases"]


def enter_kernel(ndp, names, *refs):
    r = Refs(names, refs)
    l = Links(ndp)
    nm, width = r.w4.shape[0], r.w4.shape[1]
    size = r.tokens.shape[1]
    rows = 2 * size
    heads_dev = HEADS // 4
    qk = heads_dev * HEAD_DIM
    firsts = positions(l, size)

    def place(m, s):
        return r.wa.at[s] if m == 0 else r.wall.at[m, s]

    g = Gather(l, r.w4, place, {n: r.sems("g" + n) for n in ("c", "cf", "y", "x", "z")}, width)
    tok_own = local(r.tokens.at[l.y], r.tok.at[pl.ds(0, size)], r.ld.at[0])
    wa_own = local(r.w4.at[0], r.wa.at[0], r.ld.at[1])
    copies = [local(r.w4.at[m], r.wall.at[m, 0], r.ld.at[1 + m]) for m in range(1, nm)]
    tok_own.start()
    wa_own.start()
    tok_far = remote(r.tokens.at[1 - l.y], r.tok.at[pl.ds(size, size)], *(a.at[0] for a in r.sems("tk")), l.far)
    bias_to = [
        remote(r.bias, r.biases.at[s], *(a.at[s] for a in r.sems("bi")), to)
        for s, to in ((1, l.core), (2, l.far), (3, l.cross))
    ]

    def kv_send(s):
        other = s + 1 - 2 * (s % 2)
        src = r.qkvb.at[s, pl.ds(qk, 2 * qk)]
        return remote(src, r.kvb.at[other], *(a.at[s] for a in r.sems("kv")), l.core)

    def kv_wait(s):
        other = s + 1 - 2 * (s % 2)
        src = r.qkvb.at[other, pl.ds(qk, 2 * qk)]
        return remote(src, r.kvb.at[s], *(a.at[other] for a in r.sems("kv")), l.core)

    l.greet()
    g.over_y(0).start()
    tok_far.start()
    for b in bias_to:
        b.start()
    g.core(0).start()
    r.biases[0] = r.bias[...]

    def enter(block):
        at = pl.ds(block * size, size)
        second = second_segment(firsts, size, r.kinds, block)
        x = r.tok[at].astype(F32) + jnp.where(second, r.table[1:2], r.table[0:1])
        r.xb[at] = x
        r.xl[at] = x.astype(BF)

    def project(s, block):
        at = slice(block * size, (block + 1) * size)
        column = r.biases[s].T[: 3 * qk, 0:1]
        part = dot(r.wa[s, : 3 * qk], r.xl[at], NT) + column
        r.qkvb[s, :, at] = part.astype(BF)

    tok_own.wait()
    enter(0)
    wa_own.wait()
    project(0, 0)
    fill_distance(firsts, size, r.dist)
    g.step_spread(0)
    for b in bias_to:
        b.wait_recv()
    g.core(0).wait_recv()
    project(1, 0)
    tok_far.wait_recv()
    for m in range(1, nm):
        g.over_y(m).start()
    enter(1)
    x_out = local(r.xb, r.x, r.ld.at[4])
    x_out.start()
    for s in (0, 1):
        project(s, 1)
        kv_send(s).start()
    g.step_on(0)
    for m in range(1, nm):
        g.core(m).start()
        copies[m - 1].start()
    for m in range(1, nm):
        g.step_spread(m)
    g.step_core(0)
    for m in range(1, nm):
        g.step_on(m)
    g.core_far(0).wait_recv()
    for s in (2, 3):
        project(s, 0)
        project(s, 1)
        kv_send(s).start()
    wa_out = local(r.wa, r.wall.at[0], r.ld.at[5])
    wa_out.start()

    def head(h, carry):
        s, j = h // heads_dev, h % heads_dev

        @pl.when(j == 0)
        def _():
            kv_wait(s).wait_recv()

        def lines(ref, first):
            return ref[s, pl.ds(pl.multiple_of(first + j * HEAD_DIM, HEAD_DIM), HEAD_DIM), :]

        q = lines(r.qkvb, 0) * BF(HEAD_DIM**-0.5)
        slope = r.slopes[h]
        scores = [
            dot(key, q, TN) - slope * r.dist[i * rows : (i + 1) * rows]
            for i, key in enumerate((lines(r.qkvb, qk), lines(r.kvb, 0)))
        ]
        top = jnp.maximum(*(jnp.max(a, axis=0, keepdims=True) for a in scores))
        probs = [jnp.exp(a - top) for a in scores]
        total = sum(jnp.sum(a, axis=0, keepdims=True) for a in probs)
        values = (lines(r.qkvb, 2 * qk), lines(r.kvb, qk))
        out = sum(dot(v, p.astype(BF)) for v, p in zip(values, probs))
        r.ctxb[s, pl.ds(pl.multiple_of(j * HEAD_DIM, HEAD_DIM), HEAD_DIM), :] = (out * (1.0 / total)).astype(BF)
        r.lse[pl.ds(h, 1), :] = top + jnp.log(total)
        return carry

    lax.fori_loop(0, HEADS, head, 0)
    outs = [
        local(r.qkvb, r.qkv, r.ld.at[6]),
        local(r.kvb, r.kvp, r.ld.at[7]),
        local(r.ctxb, r.ctx, r.ld.at[8]),
    ]
    for o in outs:
        o.start()
    for m in range(1, nm):
        g.step_core(m)
    for m in range(1, nm):
        g.core(m).wait_recv()
        g.core_far(m).wait_recv()
        copies[m - 1].wait()
    for m in range(nm):
        g.finish(m)
    for s in range(4):
        kv_send(s).wait_send()
    tok_far.wait_send()
    for b in bias_to:
        b.wait_send()
    for o in outs + [x_out, wa_out]:
        o.wait()


def enter_layer(ndp, tokens, w4, bias, table, kinds, slopes):
    nm, width = w4.shape[0], w4.shape[1]
    size = tokens.shape[1]
    rows = 2 * size
    qk = HEADS // 4 * HEAD_DIM
    na = ndp // 2
    n = Names()
    n.add("wa", pltpu.VMEM((4, width, width), BF))
    n.add("tok", pltpu.VMEM((rows, width), BF))
    n.add("xb", pltpu.VMEM((rows, width), F32))
    n.add("xl", pltpu.VMEM((rows, width), BF))
    n.add("qkvb", pltpu.VMEM((4, 3 * qk, rows), BF))
    n.add("kvb", pltpu.VMEM((4, 2 * qk, rows), BF))
    n.add("ctxb", pltpu.VMEM((4, qk, rows), BF))
    n.add("dist", pltpu.VMEM((2 * rows, rows), F32))
    n.add("ld", dma(9))
    n.pair("tk", 1)
    n.pair("bi", 4)
    n.pair("kv", 4)
    n.pair("gc", nm)
    n.pair("gcf", nm)
    n.pair("gy", nm)
    n.pair("gx", nm, na)
    n.pair("gz", nm, na - 1)
    shape = jax.ShapeDtypeStruct
    return pl.pallas_call(
        partial(enter_kernel, ndp, ENTER_IN + ENTER_OUT + n.names),
        in_specs=[ANY, ANY, VMEM, VMEM, SMEM, SMEM],
        out_specs=[ANY, ANY, ANY, ANY, VMEM, ANY, VMEM],
        out_shape=[
            shape((rows, width), F32),
            shape((4, 3 * qk, rows), BF),
            shape((4, 2 * qk, rows), BF),
            shape((4, qk, rows), BF),
            shape((HEADS, rows), F32),
            shape((nm, 4, width, width), BF),
            shape((4, *bias.shape), F32),
        ],
        scratch_shapes=n.shapes,
        compiler_params=pltpu.CompilerParams(
            collective_id=0, has_side_effects=True, vmem_limit_bytes=VMEM_LIMIT
        ),
    )(tokens, w4, bias, table, kinds, slopes)


LEAVE_IN = ["x", "qkv", "kvp", "ctx", "lse", "wall", "biases", "vecs", "cot", "kinds", "slopes"]
LEAVE_OUT = ["fin", "sums", "out", "gtok", "cbuf"]
B_OUT, GAIN_ONE, SHIFT_ONE, B_DOWN, GAIN_TWO, SHIFT_TWO = range(6)
DOWN, GATE, UP, ATTN = range(4)
ROW_GU, ROW_QV, SMALL_ROWS = 8, 16, 24


def leave_kernel(ndp, names, split, *refs):
    r = Refs(names, refs)
    l = Links(ndp)
    rows, width = r.x.shape
    size = rows // 2
    heads_dev = HEADS // 4
    qk = heads_dev * HEAD_DIM
    firsts = positions(l, size)
    stages = r.cstage.shape[0]
    red = Reducer(
        l,
        (r.near, r.far, r.ybuf, r.xbuf, r.zbuf, r.own, r.fin),
        {**{n: r.sems("r" + n) for n in ("y", "x", "z", "gz", "gx")}, "own": r.rown},
        width,
        split,
    )
    ticks, tail = schedule(red.units)
    small = SmallSum(l, r.smine, r.sgot, r.sems("sm"))
    sv = r.smine.at[0]

    def vec(i):
        return r.vecs[i : i + 1, :]

    def core_copy(k, i):
        src = r.cstage.at[k % stages, i]
        return remote(src, r.cbuf.at[k, i], *(a.at[k, i] for a in r.sems("co")), l.core)

    def fetch(k, i):
        return local(r.cbuf.at[k, i], r.cload, r.cl.at[0])

    def room(k, i):
        if k >= stages:
            core_copy(k - stages, i).wait_send()

    def start_fetch(k, i):
        core_copy(k, i).wait_recv()
        fetch(k, i).start()

    def merge(k, i, first, value):
        at = pl.ds(first, value.shape[0])
        total = value + r.cload[at].astype(F32)
        (r.near, r.far)[i][k, at] = total.astype(BF)

    def load_weights(s, buf):
        return local(r.wall.at[pl.ds(1, 3), s], r.wbuf.at[buf], r.wl.at[buf])

    cot_own = local(r.cot.at[l.y], r.cotb.at[pl.ds(0, size)], r.ld.at[0])
    cot_far = remote(r.cot.at[1 - l.y], r.cotb.at[pl.ds(size, size)], *(a.at[0] for a in r.sems("ct")), l.far)

    def order(i):
        return 2 * (i % 2) + i // 2

    def ffn_phase(wo, gh, a_ref, b_ref, hid, unit, hl, ht, gs, r1):
        xb, acc, gf = gh, r.gm, hl
        lx = local(r.x, xb, r.ld.at[1])
        lo = local(r.wall.at[0, pl.ds(0, 4), pl.ds(3 * qk, qk)], wo, r.ld.at[2])
        lc = local(r.ctx, r.ctxb, r.ld.at[3])
        for c in (lc, lo, lx, load_weights(0, 0), load_weights(2, 1), cot_own):
            c.start()
        l.greet()
        cot_far.start()
        red.clear_padding()
        sv[...] = jnp.zeros_like(sv)
        lc.wait()
        lo.wait()
        lx.wait()
        for s in range(4):
            part = dot(r.ctxb[s], wo[s], TN)
            if s == 0:
                acc[...] = part + xb[...] + vec(B_OUT)
            else:
                acc[...] += part
        u1, s1 = norm_forward(acc[...])
        unit[...] = u1
        r1[...] = s1
        h1 = u1 * vec(GAIN_ONE) + vec(SHIFT_ONE)
        acc[...] = h1 + vec(B_DOWN)
        hl[...] = h1.astype(BF)
        ht[...] = h1.T.astype(BF)

        def forward(i, carry):
            s, buf = order(i), i % 2
            load_weights(s, buf).wait()
            for half in range(2):
                at = slice(half * size, (half + 1) * size)
                gate = dot(hl[at], r.wbuf[buf, 0]) + r.biases[s, 1:2, :]
                up = dot(hl[at], r.wbuf[buf, 1]) + r.biases[s, 2:3, :]
                cdf, pdf = gelu_parts(gate)
                act = gate * cdf
                a_ref[s, at] = act.astype(BF)
                b_ref[s, at] = (up * (cdf + gate * pdf)).astype(BF)
                hidden = (act * up).astype(BF)
                hid[s, at] = hidden
                acc[at] += dot(hidden, r.wbuf[buf, 2])

            @pl.when(i < 2)
            def _():
                load_weights(order(i + 2), buf).start()

            return carry

        lax.fori_loop(0, 4, forward, 0)
        u2, s2 = norm_forward(acc[...])
        out = u2 * vec(GAIN_TWO) + vec(SHIFT_TWO)
        r.outb[...] = out.astype(BF)
        cot_own.wait()
        cot_far.wait_recv()
        cot = r.cotb[...].astype(F32)
        g2 = norm_backward(cot, u2, s2, vec(GAIN_TWO))
        sv[6:7, :] = jnp.sum(cot * u2, axis=0, keepdims=True)
        sv[7:8, :] = jnp.sum(cot, axis=0, keepdims=True)
        sv[5:6, :] = jnp.sum(g2, axis=0, keepdims=True)
        gh[...] = g2
        gf[...] = g2.astype(BF)
        gs[...] = g2.T.astype(BF)

        for i, s in ((1, 3), (0, 1)):
            r.cstage[DOWN % stages, i] = dot(gs[...], hid[s]).astype(BF)
            core_copy(DOWN, i).start()

        def backward(s, buf):
            load = None
            g_hidden = dot(gf[...], r.wbuf[buf, 2], NT)
            g_gate = (g_hidden * b_ref[s].astype(F32)).astype(BF)
            g_up = (g_hidden * a_ref[s].astype(F32)).astype(BF)
            row = ROW_GU + 2 * l.quarter(s)
            sv[pl.ds(row, 1), :] = jnp.sum(g_gate.astype(F32), axis=0, keepdims=True)
            sv[pl.ds(row + 1, 1), :] = jnp.sum(g_up.astype(F32), axis=0, keepdims=True)
            gh[...] += dot(g_gate, r.wbuf[buf, 0], NT)
            gh[...] += dot(g_up, r.wbuf[buf, 1], NT)
            return g_gate, g_up

        for i, s, buf in ((1, 3, 1), (0, 1, 0)):
            g_gate, g_up = backward(s, buf)
            load_weights(s - 1, buf).start()
            for k, g in ((GATE, g_gate), (UP, g_up)):
                room(k, i)
                r.cstage[k % stages, i] = dot(ht[...], g).astype(BF)
                core_copy(k, i).start()
            start_fetch(DOWN, i)
            value = dot(gs[...], hid[s - 1])
            fetch(DOWN, i).wait()
            merge(DOWN, i, 0, value)
            if i == 1:
                red.start_y(0)
                red.start_y(1)
        for i, s, buf in ((1, 2, 1), (0, 0, 0)):
            load_weights(s, buf).wait()
            g_gate, g_up = backward(s, buf)
            for k, g in ((GATE, g_gate), (UP, g_up)):
                start_fetch(k, i)
                value = dot(ht[...], g)
                fetch(k, i).wait()
                merge(k, i, 0, value)
        g_h1 = gh[...]
        unit_one = unit[...]
        sv[3:4, :] = jnp.sum(g_h1 * unit_one, axis=0, keepdims=True)
        sv[4:5, :] = jnp.sum(g_h1, axis=0, keepdims=True)
        gm = norm_backward(g_h1, unit_one, r1[...], vec(GAIN_ONE))
        sv[2:3, :] = jnp.sum(gm, axis=0, keepdims=True)
        r.gm[...] = gm
        ga = gm.astype(BF)
        r.cotb[...] = ga
        for s in range(4):
            r.gctx[s] = dot(wo[s], ga, NT).astype(BF)

    v = pltpu.VMEM
    pl.run_scoped(
        ffn_phase,
        v((4, qk, width), BF),
        v((rows, width), F32),
        v((4, rows, width), BF),
        v((4, rows, width), BF),
        v((4, rows, width), BF),
        v((rows, width), F32),
        v((rows, width), BF),
        v((width, rows), BF),
        v((width, rows), BF),
        v((rows, 1), F32),
    )

    def attention_phase(wq, qkvb, kvb, xb, xl, dist, dqkv, dkvo, dkvs):
        lq = local(r.qkv, qkvb, r.ld.at[4])
        lk = local(r.kvp, kvb, r.ld.at[5])
        lw = local(r.wall.at[0, pl.ds(0, 4), pl.ds(0, 3 * qk)], wq, r.ld.at[6])
        lx = local(r.x, xb, r.ld.at[7])
        for c in (lq, lk, lw, lx):
            c.start()
        fill_distance(firsts, size, dist)

        def other(s):
            return s + 1 - 2 * (s % 2)

        def send(s):
            return remote(dkvs.at[s], r.dkvr.at[other(s)], *(a.at[s] for a in r.sems("dk")), l.core)

        def arrived(s):
            return remote(dkvs.at[other(s)], r.dkvr.at[s], *(a.at[other(s)] for a in r.sems("dk")), l.core)

        lq.wait()
        lk.wait()

        def head(h, carry):
            s, j = h // heads_dev, h % heads_dev

            def span(first):
                return pl.ds(pl.multiple_of(first + j * HEAD_DIM, HEAD_DIM), HEAD_DIM)

            qt = qkvb[s, span(0), :] * BF(HEAD_DIM**-0.5)
            q = qt.T
            dot_t = r.gctx[s, span(0), :]
            do = dot_t.T
            slope = r.slopes[h]
            lse = r.lse[pl.ds(h, 1), :]
            keys = (qkvb[s, span(qk), :], kvb[s, span(0), :])
            values = (qkvb[s, span(2 * qk), :], kvb[s, span(qk), :])
            probs = [
                jnp.exp(dot(key, qt, TN) - slope * dist[i * rows : (i + 1) * rows] - lse)
                for i, key in enumerate(keys)
            ]
            g_probs = [dot(value, dot_t, TN) for value in values]
            inner = sum(jnp.sum(p * g, axis=0, keepdims=True) for p, g in zip(probs, g_probs))
            g_scores = [(p * (g - inner)).astype(BF) for p, g in zip(probs, g_probs)]
            dq = sum(dot(key, g) for key, g in zip(keys, g_scores))
            dqkv[s, span(0), :] = (dq * HEAD_DIM**-0.5).astype(BF)
            dk = [dot(g, q).T for g in g_scores]
            dv = [dot(p.astype(BF), do).T for p in probs]
            dkvo[s, span(0), :] = dk[0]
            dkvo[s, span(qk), :] = dv[0]
            dkvs[s, span(0), :] = dk[1].astype(BF)
            dkvs[s, span(qk), :] = dv[1].astype(BF)

            @pl.when(j == heads_dev - 1)
            def _():
                send(s).start()

            for at, steps in ticks.items():

                @pl.when(h == at)
                def _(steps=steps):
                    for name, u in steps:
                        getattr(red, name)(u)

            return carry

        lax.fori_loop(0, HEADS, head, 0)
        lw.wait()
        lx.wait()
        xl[...] = xb[...].astype(BF)
        ones = jnp.ones((8, rows), BF)
        for s in range(4):
            arrived(s).wait_recv()
            dqkv[s, qk:, :] = (dkvo[s] + r.dkvr[s].astype(F32)).astype(BF)
            g = dqkv[s]
            sv[pl.ds(ROW_QV + l.quarter(s), 1), : 3 * qk] = dot(ones, g, NT)[0:1]
            r.gm[...] += dot(g, wq[s], TN)
        g_entered = r.gm[...]
        total = jnp.sum(g_entered, axis=0, keepdims=True)
        second = sum(
            jnp.sum(
                jnp.where(second_segment(firsts, size, r.kinds, i), g_entered[i * size : (i + 1) * size], 0.0),
                axis=0,
                keepdims=True,
            )
            for i in range(2)
        )
        sv[0:1, :] = total - second
        sv[1:2, :] = second
        small.start(0)
        r.gfar[...] = g_entered[size:].astype(BF)

        def attn_parts(s):
            return ((0, dot(dqkv[s], xl[...])), (3 * qk, dot(r.ctxb[s], r.cotb[...])))

        for i, s in ((1, 3), (0, 1)):
            room(ATTN, i)
            for first, value in attn_parts(s):
                r.cstage[ATTN % stages, i, pl.ds(first, value.shape[0])] = value.astype(BF)
            core_copy(ATTN, i).start()
        small.add(0)
        for i, s in ((1, 2), (0, 0)):
            start_fetch(ATTN, i)
            parts = attn_parts(s)
            fetch(ATTN, i).wait()
            for first, value in parts:
                merge(ATTN, i, first, value)
        small.add(1)
        for s in range(4):
            send(s).wait_send()

    pl.run_scoped(
        attention_phase,
        v((4, 3 * qk, width), BF),
        v((4, 3 * qk, rows), BF),
        v((4, 2 * qk, rows), BF),
        v((rows, width), F32),
        v((rows, width), BF),
        v((2 * rows, rows), F32),
        v((4, 3 * qk, rows), BF),
        v((4, 2 * qk, rows), F32),
        v((4, 2 * qk, rows), BF),
    )

    out_own = local(r.outb.at[pl.ds(0, size)], r.out.at[l.y], r.ld.at[8])
    out_far = remote(r.outb.at[pl.ds(size, size)], r.out.at[l.y], *(a.at[0] for a in r.sems("ou")), l.far)
    tok_own = local(r.gm.at[pl.ds(0, size)], r.gtok.at[l.y], r.ld.at[9])
    tok_far = remote(r.gfar, r.ggot, *(a.at[0] for a in r.sems("gt")), l.far)
    out_own.start()
    tok_own.start()
    total = small.add(2)
    for name, u in tail:
        if name == "rows":
            out_far.start()
            tok_far.start()
        else:
            getattr(red, name)(u)
    for i in range(3, small.levels):
        total = small.add(i)
    r.sums[...] = total
    tok_far.wait_recv()
    r.gm[size:] = r.ggot[...].astype(F32)
    tok_got = local(r.gm.at[pl.ds(size, size)], r.gtok.at[1 - l.y], r.ld.at[10])
    tok_got.start()
    for u in range(red.units):
        red.finish(u)
    for k in range(4 - stages, 4):
        for i in range(2):
            core_copy(k, i).wait_send()
    small.finish()
    cot_far.wait_send()
    out_far.wait()
    tok_far.wait_send()
    for c in (out_own, tok_own, tok_got):
        c.wait()


def schedule(units):
    if units < 8:
        names = ("step_x", "step_z", "step_own", "step_on")
        first = [("start_y", u) for u in range(2, units)]
        return {}, first + [(n, u) for u in range(units) for n in names] + [("rows", 0)]
    ticks = {2: [("step_x", 0), ("step_x", 1), ("start_y", 2), ("start_y", 3)],
             5: [("step_z", 0), ("step_z", 1)],
             8: [("step_own", 0), ("step_own", 1)],
             11: [("step_on", 0), ("step_on", 1)]}
    tail = [("step_x", 2), ("start_y", 4), ("step_x", 3)]
    for u in range(4, units + 3):
        tail += [("step_z", u - 2)] if u - 2 < units else []
        tail += [("step_x", u), ("start_y", u + 1)] if u < units else []
        tail += [("rows", 0)] if u == units - 1 else []
        tail += [("step_own", u - 2)] if u - 2 < units else []
        tail += [("step_on", u - 3)] if 2 <= u - 3 < units else []
    return ticks, tail


def leave_layer(ndp, inputs, cot):
    x, wall = inputs[0], inputs[5]
    rows, width = x.shape
    nm = wall.shape[0]
    size = rows // 2
    qk = HEADS // 4 * HEAD_DIM
    na = ndp // 2
    split = 2 if width % (32 * ndp) == 0 else 1
    stages = 2 if split == 2 else 1
    units = nm * split
    cr = chunk_rows(ndp, width // split)
    padded = max(width, cr * ndp + width - width // split)
    n = Names()
    v = pltpu.VMEM
    n.add("near", v((nm, padded, width), BF))
    n.add("far", v((nm, width, width), BF))
    n.add("ybuf", v((nm, width, width), BF))
    n.add("xbuf", v((units, na, cr, width), BF))
    n.add("zbuf", v((units, na - 1, cr, width), BF))
    n.add("own", v((units, cr, width), BF))
    n.add("cstage", v((stages, 2, width, width), BF))
    n.add("cload", v((width, width), BF))
    n.add("wbuf", v((2, 3, width, width), BF))
    n.add("ctxb", v((4, qk, rows), BF))
    n.add("gctx", v((4, qk, rows), BF))
    n.add("cotb", v((rows, width), BF))
    n.add("outb", v((rows, width), BF))
    n.add("gm", v((rows, width), F32))
    n.add("gfar", v((size, width), BF))
    n.add("ggot", v((size, width), BF))
    n.add("dkvr", v((4, 2 * qk, rows), BF))
    levels = 3 + (na - 1).bit_length()
    n.add("smine", v((levels, SMALL_ROWS, width), F32))
    n.add("sgot", v((levels, SMALL_ROWS, width), F32))
    n.add("ld", dma(11))
    n.add("cl", dma(1))
    n.add("wl", dma(2))
    n.add("rown", dma(units))
    n.pair("co", nm, 2)
    n.pair("ct", 1)
    n.pair("ou", 1)
    n.pair("gt", 1)
    n.pair("dk", 4)
    n.pair("sm", levels)
    n.pair("ry", units)
    n.pair("rx", units, na)
    n.pair("rz", units, na - 1)
    n.pair("rgz", units, na - 1)
    n.pair("rgx", units, na)
    shape = jax.ShapeDtypeStruct
    return pl.pallas_call(
        partial(leave_kernel, ndp, LEAVE_IN + LEAVE_OUT + n.names, split),
        in_specs=[ANY, ANY, ANY, ANY, VMEM, ANY, VMEM, VMEM, ANY, SMEM, SMEM],
        out_specs=[ANY, VMEM, ANY, ANY, ANY],
        out_shape=[
            shape((nm, padded, width), BF),
            shape((SMALL_ROWS, width), F32),
            shape(cot.shape, BF),
            shape(cot.shape, F32),
            shape((nm, 2, width, width), BF),
        ],
        scratch_shapes=n.shapes,
        compiler_params=pltpu.CompilerParams(
            collective_id=1, has_side_effects=True, vmem_limit_bytes=VMEM_LIMIT
        ),
    )(*inputs)


def per_device(
    tokens,
    type_ids,
    boundary,
    token_type_rows,
    query_key_value_weight,
    b_qv,
    output_weight,
    b_out,
    gain_one,
    shift_one,
    gate_up_weight,
    gate_up_bias,
    down_weight,
    b_down,
    gain_two,
    shift_two,
    cotangent,
):
    nt = lax.axis_size("tensor")
    ndp = lax.axis_size("dp")
    t = lax.axis_index("tensor")
    y = t // 2
    width = tokens.shape[2]
    qk = query_key_value_weight.shape[2]
    heads_dev = qk // HEAD_DIM
    attn = jnp.concatenate(
        [query_key_value_weight.transpose(1, 2, 0).reshape(3 * qk, width), output_weight], axis=0
    )
    w4 = jnp.stack([attn, gate_up_weight[:, 0], gate_up_weight[:, 1], down_weight])
    zeros = jnp.zeros((qk,), F32)
    bias = jnp.stack([jnp.concatenate([b_qv[0], zeros, b_qv[1], zeros]), gate_up_bias[0], gate_up_bias[1]])
    bias = jnp.pad(bias, ((0, 5), (0, 0)))
    vecs = jnp.stack([b_out, gain_one, shift_one, b_down, gain_two, shift_two, b_down, b_down])
    pair = lax.dynamic_index_in_dim(type_ids, y, 0, keepdims=False)
    bound = lax.dynamic_index_in_dim(boundary, y, 0, keepdims=False)
    kinds = jnp.stack([pair[0], pair[1], bound])
    head_ids = jnp.concatenate([(t ^ s) * heads_dev + jnp.arange(heads_dev) for s in range(nt)])
    slopes = jnp.exp2(-8.0 * (head_ids + 1).astype(F32) / HEADS)

    first = enter_layer(ndp, tokens, w4, bias, token_type_rows, kinds, slopes)
    fin, sums, out, gtok, _ = leave_layer(ndp, (*first, vecs, cotangent, kinds, slopes), cotangent)
    fin = fin[:, :width].astype(F32)
    g_qkv = fin[ATTN, : 3 * qk].T.reshape(query_key_value_weight.shape)
    g_gu = jnp.stack([fin[GATE], fin[UP]], axis=1)
    g_bgu = lax.dynamic_slice_in_dim(sums, ROW_GU + 2 * t, 2, 0)
    g_bqv = lax.dynamic_index_in_dim(sums, ROW_QV + t, 0, keepdims=False)
    g_bqv = jnp.stack([g_bqv[:qk], g_bqv[2 * qk : 3 * qk]])
    return (
        out,
        gtok,
        sums[:2],
        g_qkv,
        g_bqv,
        fin[ATTN, 3 * qk :],
        sums[2],
        sums[3],
        sums[4],
        g_gu,
        g_bgu,
        fin[DOWN].T,
        sums[5],
        sums[6],
        sums[7],
    )


def solution(mesh):
    in_specs = (
        P("dp", "tensor", None),
        P("dp", None),
        P("dp"),
        P(),
        P(None, None, "tensor"),
        P(None, "tensor"),
        P("tensor", None),
        P(),
        P(),
        P(),
        P(None, None, "tensor"),
        P(None, "tensor"),
        P("tensor", None),
        P(),
        P(),
        P(),
        P("dp", "tensor", None),
    )
    out_specs = (
        P("dp", "tensor", None),
        P("dp", "tensor", None),
        P(),
        P(None, None, "tensor"),
        P(None, "tensor"),
        P("tensor", None),
        P(),
        P(),
        P(),
        P(None, None, "tensor"),
        P(None, "tensor"),
        P("tensor", None),
        P(),
        P(),
        P(),
    )
    return jax.shard_map(
        per_device, mesh=mesh, in_specs=in_specs, out_specs=out_specs, check_vma=False
    )
```

time: 863 us -> 391 us (0.45)
  waiting for transfers between devices: 514 us -> 0 us
  Pallas kernels: 0 us -> 340 us
  matrix products: 142 us -> 0 us
  blocking collectives: 66 us -> 0 us
  other arithmetic: 66.8 us -> 10.6 us
  between operations: 15.4 us -> 1.12 us
  local copies, waits for them, and re-layouts: 47.7 us -> 33.5 us
    pallas_call x0 -> x2, Pallas kernels: none -> 340 us  [the longest x1 207 us: leave_layer(): pl.pallas_call(partial(leave_kernel, ndp, LEAVE_IN + LEAVE_OUT + n.names,...]
    psum x1 -> x0, waiting for transfers between devices: 237 us -> none  [per_device(): lax.psum((grad_w_qkv, grad_b_qv, grad_w_out, grad_w_gu, grad_b_gu, grad_w...]
    reduce_scatter x8 -> x0, waiting for transfers between devices: 185 us -> none  [the longest x2 66.1 us: per_device(): lax.psum_scatter(ffn_terms, 'tensor', scatter_dimension=1, tiled=True)]
    dot_general x36 -> x0, matrix products: 133 us -> none  [the longest x2 23.5 us: per_device(): jnp.einsum('bqa,bqe->ae', hidden_reduced, feedforward_gradient, preferred...]
    all_gather x8 -> x0, waiting for transfers between devices: 91.5 us -> none  [the longest x2 34.8 us: per_device(): lax.all_gather(layer_input.astype(jnp.bfloat16), 'tensor', axis=1, tiled=...]
    psum x2 -> x0, blocking collectives: 66 us -> none  [the longest x1 43.4 us: per_device(): lax.psum((grad_table, grad_b_out, grad_gain_one, grad_shift_one, grad_b_d...]
    unnamed x208 -> x36, local copies, waits for them, and re-layouts: 44.8 us -> 15.2 us
    reduce_sum x20 -> x0, other arithmetic: 26.4 us -> none  [the longest x2 4.35 us: layer_norm(): center = jnp.mean(values, axis=-1, keepdims=True)]
  transfers between devices with their start and end apart: 17 -> 0, of which waited for: 14 -> 0; matrix products, arithmetic and copies ran while one was open for 20% -> 0% of each run, Pallas kernels for 0% -> 0%
where the time goes in v2:
time: 391 us; the launch traced here: 385 us
  Pallas kernels  340 us (87%)
  local copies, waits for them, and re-layouts  33.5 us (9%)
  other arithmetic  10.6 us (3%)
    pallas_call x1, Pallas kernels, leave_layer(): pl.pallas_call(partial(leave_kernel, ndp, LEAVE_IN + LEAVE_OUT + n.names,...  207 us
    pallas_call x1, Pallas kernels, enter_layer(): pl.pallas_call(partial(enter_kernel, ndp, ENTER_IN + ENTER_OUT + n.names)...  132 us
    unnamed x36, local copies, waits for them, and re-layouts  15.2 us

profile of v2, /device:TPU:0, one launch (start us, length us, event | category | flops | bytes accessed | tf_op | source)
XLA Modules:
  0.0 385.0 jit_solution(5504223929979588822)
XLA Ops:
  0.6 0.0 copy-start
  0.7 0.7 copy-done
  1.3 0.6 fusion.5
  1.9 1.2 dynamic_slice.16
  3.2 2.5 pad_add_fusion.refs_4_.refs_9_
  5.7 0.6 fusion.2.refs_5_.refs_10_
  6.3 6.5 %fusion.3 = (bf16[768,1,768]{2,1,0:T(2,128)(2,1)S(1)}, bf16[768,1,768]{2,1,0:T(2,128)(2,1)S(1)}) fusion(bf16[768,2,768]{2,1,0:T(2,128)(2,1)} %param.27), kind=kLoop, calls=%fused_computation.31 | loop fusion | bytes 4718592 | tf_op jit(solution)/shard_map/slice | solution.py:1005
  12.8 0.4 copy_bitcast_fusion
  13.2 0.7 copy-done.5
  14.0 0.1 copy-done.7
  14.0 0.1 maximum_bitcast_fusion
  14.1 0.5 copy-done.4
  14.6 2.7 pad_maximum_fusion.refs_1_
  17.3 0.1 pad_maximum_fusion.2
  17.4 0.6 select_maximum_fusion.refs_2_
  18.0 132.4 %shard_map.280 = (f32[512,768]{1,0:T(8,128)}, bf16[4,576,512]{2,1,0:T(8,128)(2,1)}, bf16[4,384,512]{2,1,0:T(8,128)(2,1)}, bf16[4,192,512]{2,1,0:T(8,128)(2,1)}, ...) custom-call(bf16[2,256,768]{2,1,0:T(8,128)(2,1)} %refs_0_.1, ...), custom_call_target="tpu_custom_call" | custom-call | tf_op jit(solution)/shard_map/pallas_call | solution.py:526
  150.6 0.7 stack.63.refs_7_
  151.2 207.4 %shard_map.281 = (bf16[4,768,768]{2,1,0:T(8,128)(2,1)}, f32[24,768]{1,0:T(8,128)}, bf16[2,256,768]{2,1,0:T(8,128)(2,1)}, f32[2,256,768]{2,1,0:T(8,128)}, bf16[4,2,768,768]{3,2,1,0:T(8,128)(2,1)}) custom-call(f32[512,768]{1,0:T(8,128)} %get-tuple-element.26.refs_0_, bf16[4,576,512]{2,1,0:T(8,128)(2,1)} %get-tuple-element.27.refs_1_, ...), custom_call_target="tpu_custom_call" | custom-call | tf_op jit(solution)/shard_map/pallas_call | solution.py:958
  358.7 3.2 convert_element_type.9
  361.8 0.5 slice_bitcast_fusion
  362.3 3.2 copy-done.2
  365.5 0.3 pad_maximum_fusion.1
  365.8 6.0 %copy.34 = f32[768,2,768]{2,1,0:T(2,128)} copy(f32[768,2,768]{2,0,1:T(8,128)S(1)} %pad_maximum_fusion.1) | data formatting | bytes 9437184
  371.8 1.9 copy.35
  373.8 2.0 slice_bitcast_fusion.3
  375.7 0.8 constant_dynamic-slice_fusion
  376.5 0.6 pad_maximum_fusion.3
  377.1 2.6 slice.93
  379.7 1.7 slice_reduce_fusion
  381.4 1.4 constant_dynamic-slice_fusion.1
  382.8 0.9 copy.42
  383.6 1.1 copy.43
  (38 shorter events, 0.1 us)
Async XLA Ops:
  0.6 0.7 copy-start
  12.8 1.2 copy-start.5
  12.8 1.2 copy-start.7
  13.2 1.4 copy-start.4
  14.6 2.7 copy-start.15
  14.6 2.8 copy-start.8
  18.0 132.4 %copy-start.9 = (f32[768]{0:T(1024)S(1)}, f32[768]{0:T(1024)}, u32[]{:S(2)}) copy-start(f32[768]{0:T(1024)} %param.24) | copy-start | bytes 9220
  18.0 132.4 %copy-start.10 = (f32[768]{0:T(1024)S(1)}, f32[768]{0:T(1024)}, u32[]{:S(2)}) copy-start(f32[768]{0:T(1024)} %param.25) | copy-start | bytes 9220
  18.0 132.5 %copy-start.11 = (f32[768]{0:T(1024)S(1)}, f32[768]{0:T(1024)}, u32[]{:S(2)}) copy-start(f32[768]{0:T(1024)} %param.26) | copy-start | bytes 9220
  18.0 132.5 %copy-start.12 = (f32[768]{0:T(1024)S(1)}, f32[768]{0:T(1024)}, u32[]{:S(2)}) copy-start(f32[768]{0:T(1024)} %param.30) | copy-start | bytes 9220
  18.0 132.5 %copy-start.13 = (f32[768]{0:T(1024)S(1)}, f32[768]{0:T(1024)}, u32[]{:S(2)}) copy-start(f32[768]{0:T(1024)} %param.31) | copy-start | bytes 9220
  18.0 132.5 %copy-start.14 = (f32[768]{0:T(1024)S(1)}, f32[768]{0:T(1024)}, u32[]{:S(2)}) copy-start(f32[768]{0:T(1024)} %param.32) | copy-start | bytes 9220
  361.8 3.6 copy-start.2
  373.8 9.0 %copy-start.6 = (bf16[2,256,768]{2,1,0:T(8,128)(2,1)S(1)}, bf16[2,256,768]{2,1,0:T(8,128)(2,1)}, u32[]{:S(2)}) copy-start(bf16[2,256,768]{2,1,0:T(8,128)(2,1)} %get-tuple-element.92) | copy-start | bytes 2359300
  377.1 6.5 %copy-start.3 = (f32[2,256,768]{2,1,0:T(8,128)S(1)}, f32[2,256,768]{2,1,0:T(8,128)}, u32[]{:S(2)}) copy-start(f32[2,256,768]{2,1,0:T(8,128)} %get-tuple-element.93) | copy-start | bytes 4718596
  382.8 2.0 copy-start.1
